TPU v7x, 256 devices: a whole 4x4x8 slice. The times are simulated.
256 devices in a mesh: replica: 4 (over z_lo, core), vocab: 64 (over x, y, z_hi).
Axes of the slice: x: 4, y: 4, z: 8 (z_hi: 4, z_lo: 2; z = z_hi * 2 + z_lo), core: 2. Of those that a mesh axis runs over, the one named last changes fastest.
Arguments:
- codes: bfloat16 [4, 8192, 16384], P('replica', None, 'vocab'), may hold values from -1 to 1
- block_scales: bfloat16 [4, 64, 16384], P('replica', None, 'vocab'), may hold values from 0.0055236816 to 0.05517578
- outer_head: bfloat16 [8192, 16384], P('replica', 'vocab'), may hold values from -0.1875 to 0.1875
- momentum: float32 [8192, 16384], P('replica', 'vocab'), may hold values from -0.06629126 to 0.06629126
- hidden: bfloat16 [4, 1536, 8192], P('replica', 'vocab'), may hold values from -204 to 204
- targets: int32 [4, 1536], P('replica'), may hold values from 0 to 16383
Outputs:
- loss: float32 [4, 1536], P('replica', 'vocab')
All inputs are finite; a program needn't handle non-finite values.
Results may differ from a plain program's by a relative error of at most 0.0011.
Values may be sent and summed in bfloat16 or wider, within the bound.
No kernel may reach another device: no remote copies, remote signals or barrier semaphores. Data moves between devices by JAX's collectives and lax.ppermute only.
A program may use at most 128 MiB of HBM per device.

v0:
```python
import jax
import jax.numpy as jnp
from jax import lax
from jax.sharding import PartitionSpec as P

outer_mu = 0.9
outer_lr = 0.7


def shards(codes, block_scales, outer_head, momentum, hidden, targets):
    replicas = lax.axis_size("replica")
    own_rows = outer_head.shape[0]
    width = codes.shape[2]
    block = codes.shape[1] // block_scales.shape[1]
    count = codes.shape[1]
    code_part = codes[0]
    scale_part = block_scales[0]
    term = (
        code_part.astype(jnp.float32).reshape(count // block, block, width)
        * scale_part.astype(jnp.float32)[:, None, :]
    )
    summed = lax.psum(term.reshape(count, width), "replica")
    mine = lax.dynamic_slice_in_dim(summed, lax.axis_index("replica") * own_rows, own_rows, 0)
    pseudo = mine * (1.0 / replicas)
    velocity = outer_mu * momentum + pseudo
    new_rows = (outer_head.astype(jnp.float32) - outer_lr * (pseudo + outer_mu * velocity)).astype(
        jnp.bfloat16
    )
    gathered = lax.all_gather(hidden, "vocab", axis=1, tiled=True)[0]
    tok_all = gathered.shape[0]
    logits = jnp.dot(
        gathered,
        lax.all_gather(new_rows, "replica", axis=0, tiled=True),
        preferred_element_type=jnp.float32,
    )
    local_ids = targets[0] - lax.axis_index("vocab") * width
    columns_ids = lax.broadcasted_iota(jnp.int32, (tok_all, width), 1)
    picked_local = jnp.sum(jnp.where(columns_ids == local_ids[:, None], logits, 0.0), axis=1)
    top = lax.pmax(jnp.max(logits, axis=1), "vocab")
    totals, picked = lax.psum(
        (jnp.sum(jnp.exp(logits - top[:, None]), axis=1), picked_local), "vocab"
    )
    loss_all = top + jnp.log(totals) - picked
    tok_dev = hidden.shape[1]
    mine_loss = lax.dynamic_slice_in_dim(loss_all, lax.axis_index("vocab") * tok_dev, tok_dev, 0)
    return mine_loss[None, :]


def solution(mesh):
    placed = (
        P("replica", None, "vocab"),
        P("replica", None, "vocab"),
        P("replica", "vocab"),
        P("replica", "vocab"),
        P("replica", "vocab", None),
        P("replica", None),
    )
    return jax.shard_map(
        shards, mesh=mesh, in_specs=placed, out_specs=P("replica", "vocab"), check_vma=False
    )
```

profile of v0, /device:TPU:0, one launch (start us, length us, event | category | flops | bytes accessed | tf_op | source)
XLA Modules:
  0.0 1048.6 jit_solution(10976176042612210028)
XLA Ops:
  6.5 0.0 all-reduce.3.cloned.1.call-start
  6.5 0.8 bitcast_convert_fusion
  7.3 5.9 convert_multiply_fusion
  13.2 0.0 copy-start
  13.2 0.0 copy-start.1
  13.2 0.0 all-reduce.3.cloned.1.call-update
  13.3 0.0 all-gather.3.cloned.1.call-start
  13.3 0.0 copy-start.2
  13.3 164.8 %all-reduce.3.cloned.1.call-done = f32[8192,256]{1,0:T(8,128)} async-done(((f32[8192,256]{1,0:T(8,128)}), f32[8192,256]{1,0:T(8,128)}) %all-reduce.3.cloned.1.call-update) | async-done | bytes 8388624 | tf_op jit(solution)/shard_map/psum | solution.py:22
  178.2 0.0 copy-done
  178.2 0.0 copy-done.1
  178.2 3.3 subtract_convert_fusion
  181.5 0.0 all-gather.3.cloned.1.call-update
  181.5 0.0 all-gather.5.cloned.1.call-start
  181.5 0.7 all-gather.5.cloned.1.call-update
  182.2 0.0 copy-done.2
  182.3 48.4 %all-gather.3.cloned.1.call-done = bf16[8192,256]{1,0:T(8,128)(2,1)} async-done(((bf16[2048,256]{1,0:T(8,128)(2,1)}), bf16[8192,256]{1,0:T(8,128)(2,1)}) %all-gather.3.cloned.1.call-update) | async-done | bytes 4194320 | tf_op jit(solution)/shard_map/all_gather | solution.py:33
  230.7 232.2 %all-gather.5.cloned.1.call-done = bf16[1,1536,8192]{2,1,0:T(8,128)(2,1)} async-done(((bf16[1,24,8192]{2,1,0:T(8,128)(2,1)}), bf16[1,1536,8192]{2,1,0:T(8,128)(2,1)}) %all-gather.5.cloned.1.call-update) | async-done | bytes 25165840 | tf_op jit(solution)/shard_map/all_gather | solution.py:29
  462.9 12.9 %fusion.6 = (f32[1536]{0:T(1024)S(1)}, f32[256,1536]{1,0:T(8,128)S(1)}) fusion(bf16[8192,256]{1,0:T(8,128)(2,1)} %all-gather.3.cloned.1.call-done, bf16[1,1536,8192]{2,1,0:T(8,128)(2,1)} %all-gather.5.cloned.1.call-done), kind=kOutput, calls=%fused_computation.16 | convolution fusion | flops 6442842624 | bytes 30939136 | tf_op jit(solution)/shard_map/dot_general | solution.py:31
  475.7 195.1 %pmax.7 = f32[1536]{0:T(1024)S(1)} all-reduce(f32[1536]{0:T(1024)S(1)} %get-tuple-element.9), channel_id=1, replica_groups=mesh['replica'=4,'vocab'=64] {'vocab'}, use_global_device_ids=true, to_apply=%region_2.3 | all-reduce | flops 1536 | bytes 12288 | tf_op jit(solution)/shard_map/pmax | solution.py:39
  670.9 0.4 fusion.3
  671.3 370.2 %all-reduce = (f32[1536]{0:T(1024)S(1)}, f32[1536]{0:T(1024)S(1)}) all-reduce(f32[1536]{0:T(1024)S(1)} %get-tuple-element.6, f32[1536]{0:T(1024)S(1)} %get-tuple-element.5), channel_id=1, replica_groups=mesh['replica'=4,'vocab'=64] {'vocab'}, use_global_device_ids=true, to_apply=%region_6.7 | all-reduce | flops 3072 | bytes 24576 | tf_op jit(solution)/shard_map/psum | solution.py:40
  1041.5 0.6 fusion.5
  (1 shorter events, 0.0 us)
Async XLA Ops:
  6.5 171.6 %all-reduce.3.cloned.1.call-start = ((), (), s32[]{:S(2)}) async-start(), calls=%async_computation | async-start | bytes 16777216 | tf_op jit(solution)/shard_map/psum | solution.py:22
  13.2 164.9 %copy-start = (f32[2048,256]{1,0:T(8,128)S(1)}, f32[2048,256]{1,0:T(8,128)}, u32[]{:S(2)}) copy-start(f32[2048,256]{1,0:T(8,128)} %param.9) | copy-start | bytes 6291460
  13.2 164.9 %copy-start.1 = (bf16[2048,256]{1,0:T(8,128)(2,1)S(1)}, bf16[2048,256]{1,0:T(8,128)(2,1)}, u32[]{:S(2)}) copy-start(bf16[2048,256]{1,0:T(8,128)(2,1)} %param.8) | copy-start | bytes 3145732
  13.3 217.4 %all-gather.3.cloned.1.call-start = ((), (), s32[]{:S(2)}) async-start(), calls=%async_computation.1 | async-start | bytes 5242880 | tf_op jit(solution)/shard_map/all_gather | solution.py:33
  13.3 168.9 %copy-start.2 = (s32[1,1536]{1,0:T(1,128)S(1)}, s32[1,1536]{1,0:T(1,128)}, u32[]{:S(2)}) copy-start(s32[1,1536]{1,0:T(1,128)} %param.11) | copy-start | bytes 18436
  181.5 281.4 %all-gather.5.cloned.1.call-start = ((), (), s32[]{:S(2)}) async-start(), calls=%async_computation.2 | async-start | bytes 25559040 | tf_op jit(solution)/shard_map/all_gather | solution.py:29
Sparse Core Ops, SparseCore 0:
  13.4 164.7 all-reduce.2
  181.6 49.0 all-gather.2
  234.0 228.8 all-gather.4
where the time goes:
time: 1050 us
  blocking collectives  565 us (54%)
  waiting for transfers between devices  446 us (42%)
  between operations  13.2 us (1%)
  matrix products  12.9 us (1%)
  other arithmetic  11 us (1%)
    psum x1, blocking collectives, shards(): lax.psum((jnp.sum(jnp.exp(logits - top[:, None]), axis=1), picked_local),...  370 us
    all_gather x1, waiting for transfers between devices, shards(): gathered = lax.all_gather(hidden, 'vocab', axis=1, tiled=True)[0]  232 us
    pmax x1, blocking collectives, shards(): top = lax.pmax(jnp.max(logits, axis=1), 'vocab')  195 us
    psum x1, waiting for transfers between devices, shards(): summed = lax.psum(term.reshape(count, width), 'replica')  165 us
    all_gather x1, waiting for transfers between devices, shards(): lax.all_gather(new_rows, 'replica', axis=0, tiled=True)  48.4 us
  transfers between devices with their start and end apart: 3, of which 3 were waited for; matrix products, arithmetic and copies ran while one was open for 0% of the time, Pallas kernels for 0%

commit v1 on v0

v1 whole, which is shorter than its diff:
```python
import jax
import jax.numpy as jnp
from jax import lax
from jax.sharding import Mesh, PartitionSpec as P

outer_mu = 0.9
outer_lr = 0.7

REP = ("zlo", "core")
VOC = ("x", "y", "zhi")
SWAP = [(0, 1), (1, 0)]


def shards(codes, block_scales, outer_head, momentum, hidden, targets):
    zlo = lax.axis_index("zlo")
    core = lax.axis_index("core")
    replicas = 4
    rows, width = outer_head.shape
    tok = hidden.shape[1]
    f32, bf16 = jnp.float32, jnp.bfloat16

    hid = hidden[0].reshape(tok, replicas, rows).transpose(1, 0, 2)
    hid = lax.all_to_all(hid, REP, 0, 0, tiled=True)
    hid = lax.all_gather(hid, ("y", "zhi"), axis=0, tiled=False)
    groups = hid.shape[0]
    lhs = hid.reshape(groups * replicas * tok, rows)

    blocks = block_scales.shape[1] // replicas
    per = rows // blocks
    c4 = codes.reshape(2, 2, rows, width)
    s4 = block_scales.reshape(2, 2, blocks, width)
    mine_c = lax.dynamic_index_in_dim(c4, core, 1, False)
    mine_s = lax.dynamic_index_in_dim(s4, core, 1, False)
    got_c = lax.ppermute(lax.dynamic_index_in_dim(c4, 1 - core, 1, False), "core", SWAP)
    got_s = lax.ppermute(lax.dynamic_index_in_dim(s4, 1 - core, 1, False), "core", SWAP)

    def chip_sum(z):
        def term(c, s):
            c = lax.dynamic_index_in_dim(c, z, 0, False).astype(f32)
            s = lax.dynamic_index_in_dim(s, z, 0, False).astype(f32)
            return c.reshape(blocks, per, width) * s[:, None, :]
        return (term(mine_c, mine_s) + term(got_c, got_s)).reshape(rows, width)

    other = lax.ppermute(chip_sum(1 - zlo).astype(bf16), "zlo", SWAP)
    pseudo = (chip_sum(zlo) + other.astype(f32)) * (1.0 / replicas)
    velocity = outer_mu * momentum + pseudo
    new_rows = (outer_head.astype(f32) - outer_lr * (pseudo + outer_mu * velocity)).astype(bf16)

    rhs = lax.all_gather(new_rows, "x", axis=0, tiled=False)
    nx = rhs.shape[0]
    rhs = rhs.transpose(1, 0, 2).reshape(rows, nx * width)
    part = jnp.dot(lhs, rhs, preferred_element_type=f32)

    part = part.reshape(groups, 2, 2, tok, nx * width)
    half = lax.ppermute(lax.dynamic_index_in_dim(part, 1 - core, 2, False), "core", SWAP)
    half = half + lax.dynamic_index_in_dim(part, core, 2, False)
    rest = lax.ppermute(lax.dynamic_index_in_dim(half, 1 - zlo, 1, False), "zlo", SWAP)
    logits = (rest + lax.dynamic_index_in_dim(half, zlo, 1, False)).reshape(groups * tok, nx * width)

    yz = lax.axis_index(("y", "zhi"))
    x = lax.axis_index("x")
    ids = (lax.broadcasted_iota(jnp.int32, (nx, width), 0) * groups + yz) * width
    ids = (ids + lax.broadcasted_iota(jnp.int32, (nx, width), 1)).reshape(1, nx * width)
    want = lax.dynamic_slice_in_dim(targets[0], x * groups * tok, groups * tok, 0)
    top = jnp.max(logits, axis=1)
    total = jnp.sum(jnp.exp(logits - top[:, None]), axis=1)
    picked = jnp.sum(jnp.where(ids == want[:, None], logits, 0.0), axis=1)
    stats = jnp.stack([a.reshape(groups, tok) for a in (top, total, picked)], axis=1)
    stats = lax.all_to_all(stats, ("y", "zhi"), 0, 0, tiled=True)
    top, total, picked = stats[:, 0], stats[:, 1], stats[:, 2]
    high = jnp.max(top, axis=0)
    total = jnp.sum(total * jnp.exp(top - high), axis=0)
    loss = high + jnp.log(total) - jnp.sum(picked, axis=0)
    return loss[None, :]


def solution(mesh):
    fine = Mesh(mesh.devices.reshape(2, 2, 4, 4, 4), REP + VOC)
    placed = (
        P(REP, None, VOC),
        P(REP, None, VOC),
        P(REP, VOC),
        P(REP, VOC),
        P(REP, VOC, None),
        P(REP, None),
    )
    return jax.shard_map(shards, mesh=fine, in_specs=placed, out_specs=P(REP, VOC), check_vma=False)
```

time: 1050 us -> 289 us (0.28)
  blocking collectives: 565 us -> 28 us
  waiting for transfers between devices: 446 us -> 198 us
  local copies, waits for them, and re-layouts: 0.01 us -> 18.8 us
    psum x1 -> x0, blocking collectives: 370 us -> none  [shards(): lax.psum((jnp.sum(jnp.exp(logits - top[:, None]), axis=1), picked_local),...]
    pmax x1 -> x0, blocking collectives: 195 us -> none  [shards(): top = lax.pmax(jnp.max(logits, axis=1), 'vocab')]
    psum x1 -> x0, waiting for transfers between devices: 165 us -> none  [shards(): summed = lax.psum(term.reshape(count, width), 'replica')]
    all_gather x2, waiting for transfers between devices: 281 us -> 128 us  [the longest x1 87.4 us: shards(): hid = lax.all_gather(hid, ('y', 'zhi'), axis=0, tiled=False)]
    ppermute x0 -> x5, waiting for transfers between devices: none -> 69.2 us  [the longest x1 34.8 us: shards(): lax.ppermute(lax.dynamic_index_in_dim(half, 1 - zlo, 1, False), 'zlo', SWAP)]
    all_to_all x0 -> x2, blocking collectives: none -> 28 us  [the longest x1 17.5 us: shards(): stats = lax.all_to_all(stats, ('y', 'zhi'), 0, 0, tiled=True)]
  transfers between devices with their start and end apart: 3 -> 7, of which waited for: 3 -> 7; matrix products, arithmetic and copies ran while one was open for 0% -> 2% of each run, Pallas kernels for 0% -> 0%
where the time goes in v1:
time: 289 us; the launch traced here: 287 us
  waiting for transfers between devices  198 us (69%)
  blocking collectives  28 us (10%)
  local copies, waits for them, and re-layouts  18.8 us (7%)
  between operations  13.5 us (5%)
  matrix products  11.8 us (4%)
  other arithmetic  9.32 us (3%)
  starting transfers between devices  7.96 us (3%)
    all_gather x1, waiting for transfers between devices, shards(): hid = lax.all_gather(hid, ('y', 'zhi'), axis=0, tiled=False)  87.4 us
    all_gather x1, waiting for transfers between devices, shards(): rhs = lax.all_gather(new_rows, 'x', axis=0, tiled=False)  41.1 us
    ppermute x1, waiting for transfers between devices, shards(): lax.ppermute(lax.dynamic_index_in_dim(half, 1 - zlo, 1, False), 'zlo', SWAP)  34.8 us
    ppermute x1, waiting for transfers between devices, shards(): other = lax.ppermute(chip_sum(1 - zlo).astype(bf16), 'zlo', SWAP)  25 us
    all_to_all x1, blocking collectives, shards(): stats = lax.all_to_all(stats, ('y', 'zhi'), 0, 0, tiled=True)  17.5 us
    dot_general x1, matrix products, shards(): part = jnp.dot(lhs, rhs, preferred_element_type=f32)  11.8 us
    all_to_all x1, blocking collectives, shards(): hid = lax.all_to_all(hid, REP, 0, 0, tiled=True)  10.5 us
    ppermute x1, starting transfers between devices, shards(): lax.ppermute(lax.dynamic_index_in_dim(half, 1 - zlo, 1, False), 'zlo', SWAP)  6.99 us
  transfers between devices with their start and end apart: 7, of which 7 were waited for; matrix products, arithmetic and copies ran while one was open for 2% of the time, Pallas kernels for 0%

profile of v1, /device:TPU:0, one launch (start us, length us, event | category | flops | bytes accessed | tf_op | source)
XLA Modules:
  0.0 287.1 jit_solution(962632906453930660)
XLA Ops:
  6.5 1.7 dynamic-slice_bitcast_fusion.1
  8.3 0.1 collective-permute-start
  8.4 0.5 collective-permute-start.1
  8.9 3.3 %collective-permute-done.1 = bf16[2,16,256]{2,1,0:T(8,128)(2,1)S(1)} collective-permute-done((bf16[2,16,256]{2,1,0:T(8,128)(2,1)S(1)}, bf16[2,16,256]{2,1,0:T(8,128)(2,1)S(1)}, u32[]{:S(2)}, u32[]{:S(2)}) %collective-permute-start.1) | collective-permute-done | bytes 16416 | tf_op jit(solution)/shard_map/ppermute | solution.py:35
  12.2 0.5 collective-permute-done
  12.7 1.9 fusion.1
  14.6 0.3 collective-permute-start.2
  14.9 25.0 %collective-permute-done.2 = bf16[2048,256]{1,0:T(8,128)(2,1)S(1)} collective-permute-done((bf16[2048,256]{1,0:T(8,128)(2,1)S(1)}, bf16[2048,256]{1,0:T(8,128)(2,1)S(1)}, u32[]{:S(2)}, u32[]{:S(2)}) %collective-permute-start.2) | collective-permute-done | bytes 1048608 | tf_op jit(solution)/shard_map/ppermute | solution.py:44
  39.9 3.7 %subtract_convert_fusion = bf16[2048,256]{1,0:T(8,128)(2,1)} fusion(f32[2048,256]{1,0:T(8,128)S(1)} %copy-done.2, bf16[2048,256]{1,0:T(8,128)(2,1)S(1)} %collective-permute-done.2, bf16[2048,256]{1,0:T(8,128)(2,1)S(1)} %copy-done.3, f32[16,256]{1,0:T(8,128)S(1)} %get-tuple-element.14, bf16[2,2048,256]{2,1,0:T(8,128)(2,1)} %collective-permute-done, ...), kind=kLoop, calls=%fused_computation.12 | loop fusion | flops 8388608 | bytes 7372812 | tf_op jit(solution)/shard_map/convert_element_type | solution.py:47
  43.7 0.0 all-gather.7.cloned.1.call-start
  43.7 0.3 reshape_squeeze.3
  44.0 0.2 copy.12
  44.3 10.5 %all_to_all.10 = bf16[4,24,2048]{2,1,0:T(8,128)(2,1)} all-to-all(bf16[4,24,2048]{2,1,0:T(8,128)(2,1)S(1)} %copy.12), channel_id=1, replica_groups=mesh['zlo'=2,'core'=2,'x'=4,'y'=4,'zhi'=4] {'zlo','core'}, dimensions={0} | all-to-all | bytes 786432 | tf_op jit(solution)/shard_map/all_to_all | solution.py:23
  54.8 0.0 all-gather.7.cloned.1.call-update
  54.8 41.1 %all-gather.5.cloned.1.call-done = bf16[8192,256]{1,0:T(8,128)(2,1)} async-done(((bf16[2048,256]{1,0:T(8,128)(2,1)}), bf16[8192,256]{1,0:T(8,128)(2,1)}) %all-gather.5.cloned.1.call-update) | async-done | bytes 4194320 | tf_op jit(solution)/shard_map/all_gather | solution.py:49
  95.9 6.3 %copy.11 = bf16[2048,4,256]{0,2,1:T(8,128)(2,1)} copy(bf16[2048,4,256]{2,0,1:T(8,128)(2,1)} %bitcast.76) | data formatting | bytes 8388608 | tf_op jit(solution)/shard_map/transpose | solution.py:51
  102.1 87.4 %all-gather.7.cloned.1.call-done = bf16[64,24,2048]{2,1,0:T(8,128)(2,1)} async-done(((bf16[4,24,2048]{2,1,0:T(8,128)(2,1)}), bf16[64,24,2048]{2,1,0:T(8,128)(2,1)}) %all-gather.7.cloned.1.call-update) | async-done | bytes 6291472 | tf_op jit(solution)/shard_map/all_gather | solution.py:24
  189.5 11.8 %convolution_bitcast_fusion = f32[1536,1024]{0,1:T(8,128)} fusion(bf16[2048,1024]{0,1:T(8,128)(2,1)} %bitcast.77, bf16[1536,2048]{1,0:T(8,128)(2,1)} %bitcast.91), kind=kOutput, calls=%fused_computation | convolution fusion | flops 6442450944 | bytes 16777216 | tf_op jit(solution)/shard_map/dot_general | solution.py:52
  201.3 6.6 %copy.13 = f32[1536,1024]{1,0:T(8,128)} copy(f32[1536,1024]{0,1:T(8,128)} %convolution_bitcast_fusion) | data formatting | bytes 12582912 | tf_op jit(solution)/shard_map/dot_general | solution.py:52
  207.9 2.3 dynamic-slice_bitcast_fusion
  210.2 0.1 collective-permute-start.3
  210.3 5.6 %collective-permute-done.3 = f32[16,2,24,1024]{3,2,1,0:T(8,128)S(1)} collective-permute-done((f32[16,2,24,1024]{3,2,1,0:T(8,128)S(1)}, f32[16,2,24,1024]{3,2,1,0:T(8,128)S(1)}, u32[]{:S(2)}, u32[]{:S(2)}) %collective-permute-start.3) | collective-permute-done | bytes 3145760 | tf_op jit(solution)/shard_map/ppermute | solution.py:55
  215.9 0.7 bitcast_add_fusion
  216.6 1.3 dynamic-slice_bitcast_fusion.2
  217.9 7.0 %collective-permute-start.4 = (f32[16,24,1024]{2,1,0:T(8,128)}, f32[16,24,1024]{2,1,0:T(8,128)}, u32[]{:S(2)}, u32[]{:S(2)}) collective-permute-start(f32[16,24,1024]{2,1,0:T(8,128)} %dynamic-slice_bitcast_fusion.2), channel_id=1, source_target_pairs={{0,128},{128,0},{1,129},{129,1},{2,130},{130,2},{3,131},{131,3},{4... | collective-permute-start | bytes 4718600 | tf_op jit(solution)/shard_map/ppermute | solution.py:57
  224.9 0.1 eq.17
  225.0 0.1 add_bitcast_fusion
  225.1 34.8 %collective-permute-done.4 = f32[16,24,1024]{2,1,0:T(8,128)} collective-permute-done((f32[16,24,1024]{2,1,0:T(8,128)}, f32[16,24,1024]{2,1,0:T(8,128)}, u32[]{:S(2)}, u32[]{:S(2)}) %collective-permute-start.4) | collective-permute-done | bytes 1572896 | tf_op jit(solution)/shard_map/ppermute | solution.py:57
  259.9 1.8 fusion.6
  261.6 0.5 exponential_reduce_fusion
  262.2 17.5 %all_to_all.11 = f32[16,3,24]{2,1,0:T(4,128)S(1)} all-to-all(f32[16,3,24]{2,1,0:T(4,128)S(1)} %pad_maximum_fusion), channel_id=1, replica_groups=mesh['zlo'=2,'core'=2,'x'=4,'y'=4,'zhi'=4] {'y','zhi'}, dimensions={0} | all-to-all | bytes 9216 | tf_op jit(solution)/shard_map/all_to_all | solution.py:69
  279.7 0.5 subtract_bitcast_fusion
  (24 shorter events, 0.2 us)
Async XLA Ops:
  6.5 218.3 %copy-start = (s32[1,1536]{1,0:T(1,128)S(1)}, s32[1,1536]{1,0:T(1,128)}, u32[]{:S(2)}) copy-start(s32[1,1536]{1,0:T(1,128)} %param.11) | copy-start | bytes 18436
  6.5 89.3 %all-gather.5.cloned.1.call-start = ((), (), s32[]{:S(2)}) async-start(), calls=%async_computation.2 | async-start | bytes 5242880 | tf_op jit(solution)/shard_map/all_gather | solution.py:49
  6.5 1.9 copy-start.5
  8.3 31.6 %copy-start.3 = (bf16[2048,256]{1,0:T(8,128)(2,1)S(1)}, bf16[2048,256]{1,0:T(8,128)(2,1)}, u32[]{:S(2)}) copy-start(bf16[2048,256]{1,0:T(8,128)(2,1)} %param.8) | copy-start | bytes 3145732
  8.3 4.4 %collective-permute-start = (bf16[2,2048,256]{2,1,0:T(8,128)(2,1)S(1)}, bf16[2,2048,256]{2,1,0:T(8,128)(2,1)}, u32[]{:S(2)}, u32[]{:S(2)}) collective-permute-start(bf16[2,2048,256]{2,1,0:T(8,128)(2,1)S(1)} %dynamic-slice_bitcast_fusion.1), channel_id=1, source_target_pairs={{0,64},{64,0},{1,65},{65,1},{2,66},{66,2},{3,67},{67,3},{4,68},{68... | collective-permute-start | bytes 6291464 | tf_op jit(solution)/shard_map/ppermute | solution.py:34
  8.4 3.8 %collective-permute-start.1 = (bf16[2,16,256]{2,1,0:T(8,128)(2,1)S(1)}, bf16[2,16,256]{2,1,0:T(8,128)(2,1)S(1)}, u32[]{:S(2)}, u32[]{:S(2)}) collective-permute-start(bf16[2,16,256]{2,1,0:T(8,128)(2,1)S(1)} %dynamic-slice_bitcast_fusion.3), channel_id=1, source_target_pairs={{0,64},{64,0},{1,65},{65,1},{2,66},{66,2},{3,67},{67,3},{4,68},{68... | collective-permute-start | bytes 49160 | tf_op jit(solution)/shard_map/ppermute | solution.py:35
  8.9 31.0 %copy-start.2 = (f32[2048,256]{1,0:T(8,128)S(1)}, f32[2048,256]{1,0:T(8,128)}, u32[]{:S(2)}) copy-start(f32[2048,256]{1,0:T(8,128)} %param.9) | copy-start | bytes 6291460
  14.6 25.3 %collective-permute-start.2 = (bf16[2048,256]{1,0:T(8,128)(2,1)S(1)}, bf16[2048,256]{1,0:T(8,128)(2,1)S(1)}, u32[]{:S(2)}, u32[]{:S(2)}) collective-permute-start(bf16[2048,256]{1,0:T(8,128)(2,1)S(1)} %fusion.1), channel_id=1, source_target_pairs={{0,128},{128,0},{1,129},{129,1},{2,130},{130,2},{3,131},{131,3},{4... | collective-permute-start | bytes 3145736 | tf_op jit(solution)/shard_map/ppermute | solution.py:44
  39.9 3.8 %copy-start.4 = (bf16[1,24,8192]{2,1,0:T(8,128)(2,1)S(1)}, bf16[1,24,8192]{2,1,0:T(8,128)(2,1)}, u32[]{:S(2)}) copy-start(bf16[1,24,8192]{2,1,0:T(8,128)(2,1)} %param.10) | copy-start | bytes 1179652
  43.7 145.9 %all-gather.7.cloned.1.call-start = ((), (), s32[]{:S(2)}) async-start(), calls=%async_computation.3 | async-start | bytes 6684672 | tf_op jit(solution)/shard_map/all_gather | solution.py:24
  207.9 8.0 %copy-start.1 = (f32[1536,1024]{1,0:T(8,128)S(1)}, f32[1536,1024]{1,0:T(8,128)}, u32[]{:S(2)}) copy-start(f32[1536,1024]{1,0:T(8,128)} %copy.13) | copy-start | bytes 18874372
  210.2 5.7 %collective-permute-start.3 = (f32[16,2,24,1024]{3,2,1,0:T(8,128)S(1)}, f32[16,2,24,1024]{3,2,1,0:T(8,128)S(1)}, u32[]{:S(2)}, u32[]{:S(2)}) collective-permute-start(f32[16,2,24,1024]{3,2,1,0:T(8,128)S(1)} %dynamic-slice_bitcast_fusion), channel_id=1, source_target_pairs={{0,64},{64,0},{1,65},{65,1},{2,66},{66,2},{3,67},{67,3},{4,68},{68... | collective-permute-start | bytes 9437192 | tf_op jit(solution)/shard_map/ppermute | solution.py:55
  217.9 42.0 %collective-permute-start.4 = (f32[16,24,1024]{2,1,0:T(8,128)}, f32[16,24,1024]{2,1,0:T(8,128)}, u32[]{:S(2)}, u32[]{:S(2)}) collective-permute-start(f32[16,24,1024]{2,1,0:T(8,128)} %dynamic-slice_bitcast_fusion.2), channel_id=1, source_target_pairs={{0,128},{128,0},{1,129},{129,1},{2,130},{130,2},{3,131},{131,3},{4... | collective-permute-start | bytes 4718600 | tf_op jit(solution)/shard_map/ppermute | solution.py:57
Sparse Core Ops, SparseCore 0:
  43.8 52.0 all-gather.4
  98.3 91.1 all-gather.6

commit v2 on v1

v2 whole, which is shorter than its diff:
```python
import jax
import jax.numpy as jnp
from jax import lax
from jax.sharding import Mesh, PartitionSpec as P

outer_mu = 0.9
outer_lr = 0.7

REP = ("zlo", "core")
VOC = ("x", "y", "zhi")
SWAP = [(0, 1), (1, 0)]
RING = 4


def pick(a, i, axis):
    return lax.dynamic_index_in_dim(a, i, axis, False)


def shift(a, axis, by):
    n = lax.axis_size(axis)
    return lax.ppermute(a, axis, [(i, (i + by) % n) for i in range(n)])


def after(a, *deps):
    return lax.optimization_barrier((a,) + deps)[0]


def near(a, axis):
    return shift(a, axis, 1), shift(a, axis, -1)


def far(lower, upper, axis):
    block = jnp.where(lax.axis_index("core") == 0, lower, upper)
    up = [(i, (i + 1) % RING) for i in range(RING)]
    down = [(RING + j, RING + i) for i, j in up]
    return lax.ppermute(block, ("core", axis), up + down)


def cat(*a):
    return jnp.concatenate(a, 0)


def shards(codes, block_scales, outer_head, momentum, hidden, targets):
    zlo = lax.axis_index("zlo")
    core = lax.axis_index("core")
    x = lax.axis_index("x")
    y = lax.axis_index("y")
    zhi = lax.axis_index("zhi")
    replicas = 4
    rows, width = outer_head.shape
    tok = hidden.shape[1]
    f32, bf16 = jnp.float32, jnp.bfloat16

    blocks = block_scales.shape[1] // replicas
    per = rows // blocks
    c4 = codes.reshape(2, 2, rows, width)
    s4 = block_scales.reshape(2, 2, blocks, width)
    got_c = lax.ppermute(pick(c4, 1 - core, 1), "core", SWAP)
    got_s = lax.ppermute(pick(s4, 1 - core, 1), "core", SWAP)
    mine_c = pick(c4, core, 1)
    mine_s = pick(s4, core, 1)

    hid = hidden[0].reshape(tok, replicas, rows).transpose(1, 0, 2)
    hid = lax.all_to_all(hid, REP, 0, 0, tiled=True)

    def chip_sum(z):
        def term(c, s):
            c = pick(c, z, 0).astype(f32).reshape(blocks, per, width)
            return c * pick(s, z, 0).astype(f32)[:, None, :]
        return (term(mine_c, mine_s) + term(got_c, got_s)).reshape(rows, width)

    send = chip_sum(1 - zlo).astype(bf16)
    hid = after(hid, send)
    other = lax.ppermute(send, "zlo", SWAP)
    za, zb = near(hid, "zhi")
    a0, b0 = near(hid, "y")
    f0 = far(a0, b0, "y")
    za = after(za, a0, b0)
    zf = far(za, zb, "zhi")
    mid = cat(za, zb)
    a1, b1 = near(mid, "y")
    other = after(other, za, zb)
    pseudo = (chip_sum(zlo) + other.astype(f32)) * (1.0 / replicas)
    velocity = outer_mu * momentum + pseudo
    new = (outer_head.astype(f32) - outer_lr * (pseudo + outer_mu * velocity)).astype(bf16)
    xa, xb = near(new, "x")
    f1 = far(a1, b1, "y")
    a2, b2 = near(after(zf, a1, b1), "y")
    xf = far(xa, xb, "x")
    f2 = far(a2, b2, "y")

    def stack(own, lower, upper, ends):
        n = own.shape[0] // replicas
        buf = jnp.zeros((n, 4, replicas * tok, rows), bf16)
        for dy, blk in ((0, own), (-1, lower), (1, upper), (2, ends)):
            blk = blk.reshape(n, 1, replicas * tok, rows)
            buf = lax.dynamic_update_slice(buf, blk, (0, (y + dy) % 4, 0, 0))
        return buf.reshape(n * 4 * replicas * tok, rows)

    lhs1 = cat(stack(hid, a0, b0, f0), stack(mid, a1, b1, f1))
    lhs2 = stack(zf, a2, b2, f2)

    heads = [new, xa, xb, xf]
    away = (0, -1, 1, 2)

    want = lax.dynamic_slice_in_dim(targets[0], x * 16 * tok, 16 * tok, 0).reshape(4, 4, tok)
    want = want.transpose(1, 0, 2)
    want = lax.dynamic_slice_in_dim(cat(want, want), zhi, 4, 0)
    want = jnp.stack([want[d % 4] for d in away]).reshape(16, tok)
    place = y * 4 + zhi

    def reduce_part(units):
        part = cat(*[
            jnp.dot(lhs, heads[j], preferred_element_type=f32).reshape(-1, 2, 2, tok, width)
            for _, lhs, j in units
        ])
        both = lax.ppermute(pick(part, 1 - core, 2), "core", SWAP) + pick(part, core, 2)
        rest = lax.ppermute(pick(both, 1 - zlo, 1), "zlo", SWAP)
        logits = rest + pick(both, zlo, 1)
        at = 0
        for g, lhs, j in units:
            n = lhs.shape[0] // (replicas * tok)
            part = logits[at:at + n]
            at += n
            first = (((x + away[j]) % 4) * 16 + place) * width
            ids = lax.broadcasted_iota(jnp.int32, (1, 1, width), 2) + first
            top = jnp.max(part, axis=2)
            total = jnp.sum(jnp.exp(part - top[:, :, None]), axis=2)
            hit = jnp.sum(jnp.where(ids == want[g:g + n, :, None], part, 0.0), axis=2)
            stats[g, j] = jnp.stack([top, total, hit], axis=1)

    stats = {}
    reduce_part([(0, lhs1, 0)])
    reduce_part([(0, lhs1, 1), (0, lhs1, 2)])
    reduce_part([(0, lhs1, 3)] + [(12, lhs2, j) for j in range(4)])
    table = jnp.stack([cat(stats[0, j], stats[12, j]) for j in range(4)], axis=1)
    table = table.reshape(4, 4, 12 * tok)
    table = jnp.stack([table[away.index(d)] for d in (0, 1, 2, -1)])
    table = lax.dynamic_slice_in_dim(cat(table, table), (4 - zhi) % 4, 4, 0)
    table = lax.all_to_all(table.reshape(16, 12 * tok), ("zhi", "y"), 0, 0, tiled=True)
    table = table.reshape(64, 3, tok)
    top, total, hit = table[:, 0], table[:, 1], table[:, 2]
    high = jnp.max(top, axis=0)
    total = jnp.sum(total * jnp.exp(top - high), axis=0)
    loss = high + jnp.log(total) - jnp.sum(hit, axis=0)
    return loss[None, :]


def solution(mesh):
    fine = Mesh(mesh.devices.reshape(2, 2, 4, 4, 4), REP + VOC)
    placed = (
        P(REP, None, VOC),
        P(REP, None, VOC),
        P(REP, VOC),
        P(REP, VOC),
        P(REP, VOC, None),
        P(REP, None),
    )
    return jax.shard_map(shards, mesh=fine, in_specs=placed, out_specs=P(REP, VOC), check_vma=False)
```

time: 289 us -> 179 us (0.62)
  waiting for transfers between devices: 198 us -> 103 us
  starting transfers between devices: 7.96 us -> 29.2 us
  between operations: 13.5 us -> 1.01 us
  local copies, waits for them, and re-layouts: 18.8 us -> 6.78 us
  blocking collectives: 28 us -> 16 us
  other arithmetic: 9.32 us -> 13.7 us
  matrix products: 11.8 us -> 8.07 us
    all_gather x2 -> x0, waiting for transfers between devices: 128 us -> none  [the longest x1 87.4 us: shards(): hid = lax.all_gather(hid, ('y', 'zhi'), axis=0, tiled=False)]
    ppermute x5 -> x24, waiting for transfers between devices: 69.2 us -> 99.1 us  [the longest x5 41.1 us: far(): return lax.ppermute(block, ('core', axis), up + down)]
    ppermute x5 -> x24, starting transfers between devices: 7.91 us -> 25.7 us  [the longest x10 17.7 us: shift(): return lax.ppermute(a, axis, [(i, (i + by) % n) for i in range(n)])]
    all_to_all x2 -> x1, blocking collectives: 28 us -> 16 us  [shards(): lax.all_to_all(table.reshape(16, 12 * tok), ('zhi', 'y'), 0, 0, tiled=True)]
    dot_general x1 -> x0, local copies, waits for them, and re-layouts: 6.58 us -> none  [shards(): part = jnp.dot(lhs, rhs, preferred_element_type=f32)]
    transpose x1 -> x0, local copies, waits for them, and re-layouts: 6.27 us -> none  [shards(): rhs = rhs.transpose(1, 0, 2).reshape(rows, nx * width)]
    add x1 -> x7, other arithmetic: 0.66 us -> 4.75 us  [the longest x3 4.56 us: reduce_part(): lax.ppermute(pick(part, 1 - core, 2), 'core', SWAP) + pick(part, core, 2)]
    all_to_all x0 -> x1, waiting for transfers between devices: none -> 4.04 us  [shards(): hid = lax.all_to_all(hid, REP, 0, 0, tiled=True)]
  transfers between devices with their start and end apart: 7 -> 25, of which waited for: 7 -> 13; matrix products, arithmetic and copies ran while one was open for 2% -> 13% of each run, Pallas kernels for 0% -> 0%
where the time goes in v2:
time: 179 us; the launch traced here: 178 us
  waiting for transfers between devices  103 us (58%)
  starting transfers between devices  29.2 us (16%)
  blocking collectives  16 us (9%)
  other arithmetic  13.7 us (8%)
  matrix products  8.07 us (5%)
  local copies, waits for them, and re-layouts  6.78 us (4%)
    ppermute x5, waiting for transfers between devices, far(): return lax.ppermute(block, ('core', axis), up + down)  41.1 us
    ppermute x3, waiting for transfers between devices, reduce_part(): rest = lax.ppermute(pick(both, 1 - zlo, 1), 'zlo', SWAP)  30.4 us
    ppermute x10, waiting for transfers between devices, shift(): return lax.ppermute(a, axis, [(i, (i + by) % n) for i in range(n)])  26.8 us
    ppermute x10, starting transfers between devices, shift(): return lax.ppermute(a, axis, [(i, (i + by) % n) for i in range(n)])  17.7 us
    all_to_all x1, blocking collectives, shards(): lax.all_to_all(table.reshape(16, 12 * tok), ('zhi', 'y'), 0, 0, tiled=True)  16 us
    dot_general x8, matrix products, reduce_part(): jnp.dot(lhs, heads[j], preferred_element_type=f32)  8.07 us
    add x3, other arithmetic, reduce_part(): lax.ppermute(pick(part, 1 - core, 2), 'core', SWAP) + pick(part, core, 2)  4.56 us
    ppermute x5, starting transfers between devices, far(): return lax.ppermute(block, ('core', axis), up + down)  4.21 us
  transfers between devices with their start and end apart: 25, of which 13 were waited for; matrix products, arithmetic and copies ran while one was open for 13% of the time, Pallas kernels for 0%

profile of v2, /device:TPU:0, one launch (start us, length us, event | category | flops | bytes accessed | tf_op | source)
XLA Modules:
  0.0 177.8 jit_solution(3186698570504487551)
XLA Ops:
  0.0 1.8 dynamic-slice_bitcast_fusion
  3.2 3.5 %all-to-all-start = ((bf16[4,24,2048]{2,1,0:T(8,128)(2,1)}), bf16[4,24,2048]{2,1,0:T(8,128)(2,1)S(1)}, u32[]{:S(2)}, u32[]{:S(2)}) async-start(bf16[4,24,2048]{2,1,0:T(8,128)(2,1)} %copy.36), calls=%async_computation | async-start | bytes 786432 | tf_op jit(solution)/shard_map/all_to_all | solution.py:64
  8.1 1.9 %fusion.4 = bf16[2048,256]{1,0:T(8,128)(2,1)S(1)} fusion(f32[16,256]{1,0:T(8,128)S(1)} %get-tuple-element.51, bf16[2,2048,256]{2,1,0:T(8,128)(2,1)} %collective-permute-done, s32[]{:T(128)S(6)} %select_n.198, f32[16,256]{1,0:T(8,128)S(1)} %get-tuple-element.49, bf16[2,2,2048,256]{3,2,1,0:T(8,128)(2,1)} %bitcast.166, s32[]{:T(128)S(6)} %select_n.199, ...), kind=kLoop, calls=%fused_computation.12 | loop fusion | flops 3145728 | bytes 3178508 | tf_op jit(solution)/shard_map/convert_element_type | solution.py:72
  10.0 4.0 %all-to-all-done = bf16[4,24,2048]{2,1,0:T(8,128)(2,1)S(1)} async-done(((bf16[4,24,2048]{2,1,0:T(8,128)(2,1)}), bf16[4,24,2048]{2,1,0:T(8,128)(2,1)S(1)}, u32[]{:S(2)}, u32[]{:S(2)}) %all-to-all-start) | async-done | bytes 393248 | tf_op jit(solution)/shard_map/all_to_all | solution.py:64
  14.1 3.2 %collective-permute-start.3 = (bf16[4,24,2048]{2,1,0:T(8,128)(2,1)S(1)}, bf16[4,24,2048]{2,1,0:T(8,128)(2,1)S(1)}, u32[]{:S(2)}, u32[]{:S(2)}) collective-permute-start(bf16[4,24,2048]{2,1,0:T(8,128)(2,1)S(1)} %all-to-all-done), channel_id=1, source_target_pairs={{0,12},{4,0},{8,4},{12,8},{1,13},{5,1},{9,5},{13,9},{2,14},{6,2},{... | collective-permute-start | bytes 1179656 | tf_op jit(solution)/shard_map/ppermute | solution.py:21
  17.3 1.8 collective-permute-start.5
  19.2 2.9 %collective-permute-start.6 = (bf16[4,24,2048]{2,1,0:T(8,128)(2,1)S(1)}, bf16[4,24,2048]{2,1,0:T(8,128)(2,1)S(1)}, u32[]{:S(2)}, u32[]{:S(2)}) collective-permute-start(bf16[4,24,2048]{2,1,0:T(8,128)(2,1)S(1)} %all-to-all-done), channel_id=1, source_target_pairs={{0,3},{1,0},{2,1},{3,2},{4,7},{5,4},{6,5},{7,6},{8,11},{9,8},{10,9... | collective-permute-start | bytes 1179656 | tf_op jit(solution)/shard_map/ppermute | solution.py:21
  22.7 3.3 %collective-permute-done.2 = bf16[4,24,2048]{2,1,0:T(8,128)(2,1)S(1)} collective-permute-done((bf16[4,24,2048]{2,1,0:T(8,128)(2,1)S(1)}, bf16[4,24,2048]{2,1,0:T(8,128)(2,1)S(1)}, u32[]{:S(2)}, u32[]{:S(2)}) %collective-permute-start.2) | collective-permute-done | bytes 393248 | tf_op jit(solution)/shard_map/ppermute | solution.py:21
  25.9 14.3 %collective-permute-done.5 = bf16[4,24,2048]{2,1,0:T(8,128)(2,1)S(1)} collective-permute-done((bf16[4,24,2048]{2,1,0:T(8,128)(2,1)S(1)}, bf16[4,24,2048]{2,1,0:T(8,128)(2,1)S(1)}, u32[]{:S(2)}, u32[]{:S(2)}) %collective-permute-start.5) | collective-permute-done | bytes 393248 | tf_op jit(solution)/shard_map/ppermute | solution.py:21
  40.7 2.9 %collective-permute-start.8 = (bf16[8,24,2048]{2,1,0:T(8,128)(2,1)S(1)}, bf16[8,24,2048]{2,1,0:T(8,128)(2,1)S(1)}, u32[]{:S(2)}, u32[]{:S(2)}) collective-permute-start(bf16[8,24,2048]{2,1,0:T(8,128)(2,1)S(1)} %get-tuple-element.40), channel_id=1, source_target_pairs={{0,12},{4,0},{8,4},{12,8},{1,13},{5,1},{9,5},{13,9},{2,14},{6,2},{... | collective-permute-start | bytes 2359304 | tf_op jit(solution)/shard_map/ppermute | solution.py:21
  43.7 2.5 %collective-permute-start.16 = (bf16[4,24,2048]{2,1,0:T(8,128)(2,1)S(1)}, bf16[4,24,2048]{2,1,0:T(8,128)(2,1)S(1)}, u32[]{:S(2)}, u32[]{:S(2)}) collective-permute-start(bf16[4,24,2048]{2,1,0:T(8,128)(2,1)S(1)} %get-tuple-element.39), channel_id=1, source_target_pairs={{0,1},{1,2},{2,3},{3,0},{65,64},{66,65},{67,66},{64,67},{4,5},{5,6... | collective-permute-start | bytes 1179656 | tf_op jit(solution)/shard_map/ppermute | solution.py:36
  46.9 22.9 %collective-permute-done.16 = bf16[4,24,2048]{2,1,0:T(8,128)(2,1)S(1)} collective-permute-done((bf16[4,24,2048]{2,1,0:T(8,128)(2,1)S(1)}, bf16[4,24,2048]{2,1,0:T(8,128)(2,1)S(1)}, u32[]{:S(2)}, u32[]{:S(2)}) %collective-permute-start.16) | collective-permute-done | bytes 393248 | tf_op jit(solution)/shard_map/ppermute | solution.py:36
  70.0 2.7 %subtract_convert_fusion = bf16[2048,256]{1,0:T(8,128)(2,1)S(1)} fusion(f32[2048,256]{1,0:T(8,128)S(1)} %copy-done.5, bf16[2048,256]{1,0:T(8,128)(2,1)S(1)} %collective-permute-done.10, bf16[2048,256]{1,0:T(8,128)(2,1)S(1)} %copy-done.7, f32[16,256]{1,0:T(8,128)S(1)} %get-tuple-element.50, bf16[2,2048,256]{2,1,0:T(8,128)(2,1)} %collective-permute-done, ...), kind=kLoop, calls=%fused_computation.14 | loop fusion | flops 8388608 | bytes 7372812 | tf_op jit(solution)/shard_map/convert_element_type | solution.py:85
  72.8 1.6 collective-permute-start.13
  74.3 1.7 collective-permute-start.14
  76.4 2.9 %collective-permute-start.18 = (bf16[4,24,2048]{2,1,0:T(8,128)(2,1)S(1)}, bf16[4,24,2048]{2,1,0:T(8,128)(2,1)S(1)}, u32[]{:S(2)}, u32[]{:S(2)}) collective-permute-start(bf16[4,24,2048]{2,1,0:T(8,128)(2,1)S(1)} %collective-permute-done.16), channel_id=1, source_target_pairs={{0,12},{4,0},{8,4},{12,8},{1,13},{5,1},{9,5},{13,9},{2,14},{6,2},{... | collective-permute-start | bytes 1179656 | tf_op jit(solution)/shard_map/ppermute | solution.py:21
  79.6 5.4 %collective-permute-done.17 = bf16[4,24,2048]{2,1,0:T(8,128)(2,1)S(1)} collective-permute-done((bf16[4,24,2048]{2,1,0:T(8,128)(2,1)S(1)}, bf16[4,24,2048]{2,1,0:T(8,128)(2,1)S(1)}, u32[]{:S(2)}, u32[]{:S(2)}) %collective-permute-start.17) | collective-permute-done | bytes 393248 | tf_op jit(solution)/shard_map/ppermute | solution.py:21
  85.1 3.8 %collective-permute-done.18 = bf16[4,24,2048]{2,1,0:T(8,128)(2,1)S(1)} collective-permute-done((bf16[4,24,2048]{2,1,0:T(8,128)(2,1)S(1)}, bf16[4,24,2048]{2,1,0:T(8,128)(2,1)S(1)}, u32[]{:S(2)}, u32[]{:S(2)}) %collective-permute-start.18) | collective-permute-done | bytes 393248 | tf_op jit(solution)/shard_map/ppermute | solution.py:21
  90.2 3.3 %collective-permute-done.9 = bf16[8,24,2048]{2,1,0:T(8,128)(2,1)S(1)} collective-permute-done((bf16[8,24,2048]{2,1,0:T(8,128)(2,1)S(1)}, bf16[8,24,2048]{2,1,0:T(8,128)(2,1)S(1)}, u32[]{:S(2)}, u32[]{:S(2)}) %collective-permute-start.9) | collective-permute-done | bytes 786464 | tf_op jit(solution)/shard_map/ppermute | solution.py:36
  93.6 1.4 fusion.27
  95.2 3.3 %collective-permute-done.19 = bf16[4,24,2048]{2,1,0:T(8,128)(2,1)S(1)} collective-permute-done((bf16[4,24,2048]{2,1,0:T(8,128)(2,1)S(1)}, bf16[4,24,2048]{2,1,0:T(8,128)(2,1)S(1)}, u32[]{:S(2)}, u32[]{:S(2)}) %collective-permute-start.19) | collective-permute-done | bytes 393248 | tf_op jit(solution)/shard_map/ppermute | solution.py:36
  99.0 1.4 fusion.24
  103.1 11.6 %collective-permute-done.15 = bf16[2048,256]{1,0:T(8,128)(2,1)S(1)} collective-permute-done((bf16[2048,256]{1,0:T(8,128)(2,1)S(1)}, bf16[2048,256]{1,0:T(8,128)(2,1)S(1)}, u32[]{:S(2)}, u32[]{:S(2)}) %collective-permute-start.15) | collective-permute-done | bytes 1048608 | tf_op jit(solution)/shard_map/ppermute | solution.py:36
  114.7 1.4 fusion.26
  120.2 1.5 bitcast_add_fusion.3
  122.1 1.5 fusion.7
  123.7 1.8 collective-permute-start.23
  125.4 1.6 bitcast_add_fusion
  127.6 4.0 %collective-permute-done.12 = f32[12,24,256]{2,1,0:T(8,128)S(1)} collective-permute-done((f32[12,24,256]{2,1,0:T(8,128)S(1)}, f32[12,24,256]{2,1,0:T(8,128)S(1)}, u32[]{:S(2)}, u32[]{:S(2)}) %collective-permute-start.12) | collective-permute-done | bytes 294944 | tf_op jit(solution)/shard_map/ppermute | solution.py:118
  131.7 12.5 %collective-permute-done.23 = f32[24,24,256]{2,1,0:T(8,128)S(1)} collective-permute-done((f32[24,24,256]{2,1,0:T(8,128)S(1)}, f32[24,24,256]{2,1,0:T(8,128)S(1)}, u32[]{:S(2)}, u32[]{:S(2)}) %collective-permute-start.23) | collective-permute-done | bytes 589856 | tf_op jit(solution)/shard_map/ppermute | solution.py:118
  144.7 13.9 %collective-permute-done.21 = f32[28,24,256]{2,1,0:T(8,128)S(1)} collective-permute-done((f32[28,24,256]{2,1,0:T(8,128)S(1)}, f32[28,24,256]{2,1,0:T(8,128)S(1)}, u32[]{:S(2)}, u32[]{:S(2)}) %collective-permute-start.21) | collective-permute-done | bytes 688160 | tf_op jit(solution)/shard_map/ppermute | solution.py:118
  160.9 16.0 %all_to_all.14 = f32[16,1,288]{2,1,0:T(1,128)S(1)} all-to-all(f32[16,1,288]{2,1,0:T(1,128)S(1)} %all_to_all.10), channel_id=1, replica_groups=mesh['zlo'=2,'core'=2,'x'=4,'y'=4,'zhi'=4] {'zhi','y'}, dimensions={0} | all-to-all | bytes 36864 | tf_op jit(solution)/shard_map/all_to_all | solution.py:140
  (152 shorter events, 18.7 us)
Async XLA Ops:
  0.0 19.1 %copy-start = (s32[1,1536]{1,0:T(1,128)S(1)}, s32[1,1536]{1,0:T(1,128)}, u32[]{:S(2)}) copy-start(s32[1,1536]{1,0:T(1,128)} %param.11) | copy-start | bytes 18436
  1.8 4.9 %copy-start.9 = (bf16[1,64,256]{2,1,0:T(8,128)(2,1)S(1)}, bf16[1,64,256]{2,1,0:T(8,128)(2,1)}, u32[]{:S(2)}) copy-start(bf16[1,64,256]{2,1,0:T(8,128)(2,1)} %param.7) | copy-start | bytes 98308
  1.8 6.3 %collective-permute-start = (bf16[2,2048,256]{2,1,0:T(8,128)(2,1)S(1)}, bf16[2,2048,256]{2,1,0:T(8,128)(2,1)}, u32[]{:S(2)}, u32[]{:S(2)}) collective-permute-start(bf16[2,2048,256]{2,1,0:T(8,128)(2,1)S(1)} %dynamic-slice_bitcast_fusion), channel_id=1, source_target_pairs={{0,64},{64,0},{1,65},{65,1},{2,66},{66,2},{3,67},{67,3},{4,68},{68... | collective-permute-start | bytes 6291464 | tf_op jit(solution)/shard_map/ppermute | solution.py:58
  3.2 10.9 %all-to-all-start = ((bf16[4,24,2048]{2,1,0:T(8,128)(2,1)}), bf16[4,24,2048]{2,1,0:T(8,128)(2,1)S(1)}, u32[]{:S(2)}, u32[]{:S(2)}) async-start(bf16[4,24,2048]{2,1,0:T(8,128)(2,1)} %copy.36), calls=%async_computation | async-start | bytes 786432 | tf_op jit(solution)/shard_map/all_to_all | solution.py:64
  6.7 1.4 collective-permute-start.1
  14.1 11.9 %collective-permute-start.2 = (bf16[4,24,2048]{2,1,0:T(8,128)(2,1)S(1)}, bf16[4,24,2048]{2,1,0:T(8,128)(2,1)S(1)}, u32[]{:S(2)}, u32[]{:S(2)}) collective-permute-start(bf16[4,24,2048]{2,1,0:T(8,128)(2,1)S(1)} %all-to-all-done), channel_id=1, source_target_pairs={{0,4},{4,8},{8,12},{12,0},{1,5},{5,9},{9,13},{13,1},{2,6},{6,10},{... | collective-permute-start | bytes 1179656 | tf_op jit(solution)/shard_map/ppermute | solution.py:21
  14.1 11.8 %collective-permute-start.3 = (bf16[4,24,2048]{2,1,0:T(8,128)(2,1)S(1)}, bf16[4,24,2048]{2,1,0:T(8,128)(2,1)S(1)}, u32[]{:S(2)}, u32[]{:S(2)}) collective-permute-start(bf16[4,24,2048]{2,1,0:T(8,128)(2,1)S(1)} %all-to-all-done), channel_id=1, source_target_pairs={{0,12},{4,0},{8,4},{12,8},{1,13},{5,1},{9,5},{13,9},{2,14},{6,2},{... | collective-permute-start | bytes 1179656 | tf_op jit(solution)/shard_map/ppermute | solution.py:21
  17.3 22.9 %collective-permute-start.5 = (bf16[4,24,2048]{2,1,0:T(8,128)(2,1)S(1)}, bf16[4,24,2048]{2,1,0:T(8,128)(2,1)S(1)}, u32[]{:S(2)}, u32[]{:S(2)}) collective-permute-start(bf16[4,24,2048]{2,1,0:T(8,128)(2,1)S(1)} %all-to-all-done), channel_id=1, source_target_pairs={{0,1},{1,2},{2,3},{3,0},{4,5},{5,6},{6,7},{7,4},{8,9},{9,10},{10,1... | collective-permute-start | bytes 1179656 | tf_op jit(solution)/shard_map/ppermute | solution.py:21
  19.2 21.0 %collective-permute-start.6 = (bf16[4,24,2048]{2,1,0:T(8,128)(2,1)S(1)}, bf16[4,24,2048]{2,1,0:T(8,128)(2,1)S(1)}, u32[]{:S(2)}, u32[]{:S(2)}) collective-permute-start(bf16[4,24,2048]{2,1,0:T(8,128)(2,1)S(1)} %all-to-all-done), channel_id=1, source_target_pairs={{0,3},{1,0},{2,1},{3,2},{4,7},{5,4},{6,5},{7,6},{8,11},{9,8},{10,9... | collective-permute-start | bytes 1179656 | tf_op jit(solution)/shard_map/ppermute | solution.py:21
  22.1 47.9 %collective-permute-start.10 = (bf16[2048,256]{1,0:T(8,128)(2,1)S(1)}, bf16[2048,256]{1,0:T(8,128)(2,1)S(1)}, u32[]{:S(2)}, u32[]{:S(2)}) collective-permute-start(bf16[2048,256]{1,0:T(8,128)(2,1)S(1)} %fusion.4), channel_id=1, source_target_pairs={{0,128},{128,0},{1,129},{129,1},{2,130},{130,2},{3,131},{131,3},{4... | collective-permute-start | bytes 3145736 | tf_op jit(solution)/shard_map/ppermute | solution.py:74
  40.3 35.7 %collective-permute-start.7 = (bf16[8,24,2048]{2,1,0:T(8,128)(2,1)S(1)}, bf16[8,24,2048]{2,1,0:T(8,128)(2,1)S(1)}, u32[]{:S(2)}, u32[]{:S(2)}) collective-permute-start(bf16[8,24,2048]{2,1,0:T(8,128)(2,1)S(1)} %get-tuple-element.40), channel_id=1, source_target_pairs={{0,4},{4,8},{8,12},{12,0},{1,5},{5,9},{9,13},{13,1},{2,6},{6,10},{... | collective-permute-start | bytes 2359304 | tf_op jit(solution)/shard_map/ppermute | solution.py:21
  40.7 35.3 %collective-permute-start.8 = (bf16[8,24,2048]{2,1,0:T(8,128)(2,1)S(1)}, bf16[8,24,2048]{2,1,0:T(8,128)(2,1)S(1)}, u32[]{:S(2)}, u32[]{:S(2)}) collective-permute-start(bf16[8,24,2048]{2,1,0:T(8,128)(2,1)S(1)} %get-tuple-element.40), channel_id=1, source_target_pairs={{0,12},{4,0},{8,4},{12,8},{1,13},{5,1},{9,5},{13,9},{2,14},{6,2},{... | collective-permute-start | bytes 2359304 | tf_op jit(solution)/shard_map/ppermute | solution.py:21
  43.7 26.1 %collective-permute-start.16 = (bf16[4,24,2048]{2,1,0:T(8,128)(2,1)S(1)}, bf16[4,24,2048]{2,1,0:T(8,128)(2,1)S(1)}, u32[]{:S(2)}, u32[]{:S(2)}) collective-permute-start(bf16[4,24,2048]{2,1,0:T(8,128)(2,1)S(1)} %get-tuple-element.39), channel_id=1, source_target_pairs={{0,1},{1,2},{2,3},{3,0},{65,64},{66,65},{67,66},{64,67},{4,5},{5,6... | collective-permute-start | bytes 1179656 | tf_op jit(solution)/shard_map/ppermute | solution.py:36
  46.2 23.8 %collective-permute-start.4 = (bf16[4,24,2048]{2,1,0:T(8,128)(2,1)S(1)}, bf16[4,24,2048]{2,1,0:T(8,128)(2,1)S(1)}, u32[]{:S(2)}, u32[]{:S(2)}) collective-permute-start(bf16[4,24,2048]{2,1,0:T(8,128)(2,1)S(1)} %broadcast_select_fusion.4), channel_id=1, source_target_pairs={{0,4},{4,8},{8,12},{12,0},{68,64},{72,68},{76,72},{64,76},{1,5},{5... | collective-permute-start | bytes 1179656 | tf_op jit(solution)/shard_map/ppermute | solution.py:36
  46.8 23.2 %copy-start.5 = (f32[2048,256]{1,0:T(8,128)S(1)}, f32[2048,256]{1,0:T(8,128)}, u32[]{:S(2)}) copy-start(f32[2048,256]{1,0:T(8,128)} %param.9) | copy-start | bytes 6291460
  46.8 23.2 %copy-start.7 = (bf16[2048,256]{1,0:T(8,128)(2,1)S(1)}, bf16[2048,256]{1,0:T(8,128)(2,1)}, u32[]{:S(2)}) copy-start(bf16[2048,256]{1,0:T(8,128)(2,1)} %param.8) | copy-start | bytes 3145732
  72.8 25.7 %collective-permute-start.13 = (bf16[2048,256]{1,0:T(8,128)(2,1)S(1)}, bf16[2048,256]{1,0:T(8,128)(2,1)S(1)}, u32[]{:S(2)}, u32[]{:S(2)}) collective-permute-start(bf16[2048,256]{1,0:T(8,128)(2,1)S(1)} %subtract_convert_fusion), channel_id=1, source_target_pairs={{0,16},{16,32},{32,48},{48,0},{1,17},{17,33},{33,49},{49,1},{2,18}... | collective-permute-start | bytes 3145736 | tf_op jit(solution)/shard_map/ppermute | solution.py:21
  74.3 24.2 %collective-permute-start.14 = (bf16[2048,256]{1,0:T(8,128)(2,1)S(1)}, bf16[2048,256]{1,0:T(8,128)(2,1)S(1)}, u32[]{:S(2)}, u32[]{:S(2)}) collective-permute-start(bf16[2048,256]{1,0:T(8,128)(2,1)S(1)} %subtract_convert_fusion), channel_id=1, source_target_pairs={{0,48},{16,0},{32,16},{48,32},{1,49},{17,1},{33,17},{49,33},{2,50}... | collective-permute-start | bytes 3145736 | tf_op jit(solution)/shard_map/ppermute | solution.py:21
  76.1 9.0 %collective-permute-start.17 = (bf16[4,24,2048]{2,1,0:T(8,128)(2,1)S(1)}, bf16[4,24,2048]{2,1,0:T(8,128)(2,1)S(1)}, u32[]{:S(2)}, u32[]{:S(2)}) collective-permute-start(bf16[4,24,2048]{2,1,0:T(8,128)(2,1)S(1)} %collective-permute-done.16), channel_id=1, source_target_pairs={{0,4},{4,8},{8,12},{12,0},{1,5},{5,9},{9,13},{13,1},{2,6},{6,10},{... | collective-permute-start | bytes 1179656 | tf_op jit(solution)/shard_map/ppermute | solution.py:21
  76.4 12.5 %collective-permute-start.18 = (bf16[4,24,2048]{2,1,0:T(8,128)(2,1)S(1)}, bf16[4,24,2048]{2,1,0:T(8,128)(2,1)S(1)}, u32[]{:S(2)}, u32[]{:S(2)}) collective-permute-start(bf16[4,24,2048]{2,1,0:T(8,128)(2,1)S(1)} %collective-permute-done.16), channel_id=1, source_target_pairs={{0,12},{4,0},{8,4},{12,8},{1,13},{5,1},{9,5},{13,9},{2,14},{6,2},{... | collective-permute-start | bytes 1179656 | tf_op jit(solution)/shard_map/ppermute | solution.py:21
  79.4 14.1 %collective-permute-start.9 = (bf16[8,24,2048]{2,1,0:T(8,128)(2,1)S(1)}, bf16[8,24,2048]{2,1,0:T(8,128)(2,1)S(1)}, u32[]{:S(2)}, u32[]{:S(2)}) collective-permute-start(bf16[8,24,2048]{2,1,0:T(8,128)(2,1)S(1)} %broadcast_select_fusion.1), channel_id=1, source_target_pairs={{0,4},{4,8},{8,12},{12,0},{68,64},{72,68},{76,72},{64,76},{1,5},{5... | collective-permute-start | bytes 2359304 | tf_op jit(solution)/shard_map/ppermute | solution.py:36
  88.9 9.5 %collective-permute-start.19 = (bf16[4,24,2048]{2,1,0:T(8,128)(2,1)S(1)}, bf16[4,24,2048]{2,1,0:T(8,128)(2,1)S(1)}, u32[]{:S(2)}, u32[]{:S(2)}) collective-permute-start(bf16[4,24,2048]{2,1,0:T(8,128)(2,1)S(1)} %broadcast_select_fusion.2), channel_id=1, source_target_pairs={{0,4},{4,8},{8,12},{12,0},{68,64},{72,68},{76,72},{64,76},{1,5},{5... | collective-permute-start | bytes 1179656 | tf_op jit(solution)/shard_map/ppermute | solution.py:36
  95.0 3.7 %copy-start.6 = (f32[1152,256]{1,0:T(8,128)}, f32[1152,256]{1,0:T(8,128)S(1)}, u32[]{:S(2)}) copy-start(f32[1152,256]{1,0:T(8,128)S(1)} %fusion.27) | copy-start | bytes 3538948
  95.1 25.1 %collective-permute-start.11 = (f32[12,2,24,256]{3,2,1,0:T(8,128)S(1)}, f32[12,2,24,256]{3,2,1,0:T(8,128)}, u32[]{:S(2)}, u32[]{:S(2)}) collective-permute-start(f32[12,2,24,256]{3,2,1,0:T(8,128)S(1)} %dynamic-slice_bitcast_fusion.4), channel_id=1, source_target_pairs={{0,64},{64,0},{1,65},{65,1},{2,66},{66,2},{3,67},{67,3},{4,68},{68... | collective-permute-start | bytes 1769480 | tf_op jit(solution)/shard_map/ppermute | solution.py:117
  98.6 16.1 %collective-permute-start.15 = (bf16[2048,256]{1,0:T(8,128)(2,1)S(1)}, bf16[2048,256]{1,0:T(8,128)(2,1)S(1)}, u32[]{:S(2)}, u32[]{:S(2)}) collective-permute-start(bf16[2048,256]{1,0:T(8,128)(2,1)S(1)} %broadcast_select_fusion), channel_id=1, source_target_pairs={{0,16},{16,32},{32,48},{48,0},{80,64},{96,80},{112,96},{64,112},{1... | collective-permute-start | bytes 3145736 | tf_op jit(solution)/shard_map/ppermute | solution.py:36
  101.8 14.3 %copy-start.3 = (f32[1152,256]{1,0:T(8,128)}, f32[1152,256]{1,0:T(8,128)S(1)}, u32[]{:S(2)}) copy-start(f32[1152,256]{1,0:T(8,128)S(1)} %fusion.25) | copy-start | bytes 3538948
  103.1 19.0 %collective-permute-start.22 = (f32[24,2,24,256]{3,2,1,0:T(8,128)}, f32[24,2,24,256]{3,2,1,0:T(8,128)}, u32[]{:S(2)}, u32[]{:S(2)}) collective-permute-start(f32[24,2,24,256]{3,2,1,0:T(8,128)} %fusion.9), channel_id=1, source_target_pairs={{0,64},{64,0},{1,65},{65,1},{2,66},{66,2},{3,67},{67,3},{4,68},{68... | collective-permute-start | bytes 3538952 | tf_op jit(solution)/shard_map/ppermute | solution.py:117
  119.9 5.5 %collective-permute-start.20 = (f32[28,2,24,256]{3,2,1,0:T(8,128)}, f32[28,2,24,256]{3,2,1,0:T(8,128)}, u32[]{:S(2)}, u32[]{:S(2)}) collective-permute-start(f32[28,2,24,256]{3,2,1,0:T(8,128)} %dynamic-slice_bitcast_fusion.1), channel_id=1, source_target_pairs={{0,64},{64,0},{1,65},{65,1},{2,66},{66,2},{3,67},{67,3},{4,68},{68... | collective-permute-start | bytes 4128776 | tf_op jit(solution)/shard_map/ppermute | solution.py:117
  120.1 2.0 %copy-start.2 = (f32[1152,256]{1,0:T(8,128)S(1)}, f32[1152,256]{1,0:T(8,128)}, u32[]{:S(2)}) copy-start(f32[1152,256]{1,0:T(8,128)} %copy-done.1) | copy-start | bytes 3538948
  121.7 9.9 %collective-permute-start.12 = (f32[12,24,256]{2,1,0:T(8,128)S(1)}, f32[12,24,256]{2,1,0:T(8,128)S(1)}, u32[]{:S(2)}, u32[]{:S(2)}) collective-permute-start(f32[12,24,256]{2,1,0:T(8,128)S(1)} %dynamic-slice_bitcast_fusion.5), channel_id=1, source_target_pairs={{0,128},{128,0},{1,129},{129,1},{2,130},{130,2},{3,131},{131,3},{4... | collective-permute-start | bytes 884744 | tf_op jit(solution)/shard_map/ppermute | solution.py:118
  123.7 20.6 %collective-permute-start.23 = (f32[24,24,256]{2,1,0:T(8,128)S(1)}, f32[24,24,256]{2,1,0:T(8,128)S(1)}, u32[]{:S(2)}, u32[]{:S(2)}) collective-permute-start(f32[24,24,256]{2,1,0:T(8,128)S(1)} %dynamic-slice_bitcast_fusion.3), channel_id=1, source_target_pairs={{0,128},{128,0},{1,129},{129,1},{2,130},{130,2},{3,131},{131,3},{4... | collective-permute-start | bytes 1769480 | tf_op jit(solution)/shard_map/ppermute | solution.py:118
  127.1 31.5 %collective-permute-start.21 = (f32[28,24,256]{2,1,0:T(8,128)S(1)}, f32[28,24,256]{2,1,0:T(8,128)S(1)}, u32[]{:S(2)}, u32[]{:S(2)}) collective-permute-start(f32[28,24,256]{2,1,0:T(8,128)S(1)} %dynamic-slice_bitcast_fusion.2), channel_id=1, source_target_pairs={{0,128},{128,0},{1,129},{129,1},{2,130},{130,2},{3,131},{131,3},{4... | collective-permute-start | bytes 2064392 | tf_op jit(solution)/shard_map/ppermute | solution.py:118
  (3 other events, 5.4 us)

commit v3 on v2

--- a/solution.py
+++ b/solution.py
@@ -30,10 +30,13 @@
 
 
 def far(lower, upper, axis):
-    block = jnp.where(lax.axis_index("core") == 0, lower, upper)
+    return onward(jnp.where(lax.axis_index("core") == 0, lower, upper), axis)
+
+
+def onward(a, axis):
     up = [(i, (i + 1) % RING) for i in range(RING)]
     down = [(RING + j, RING + i) for i, j in up]
-    return lax.ppermute(block, ("core", axis), up + down)
+    return lax.ppermute(a, ("core", axis), up + down)
 
 
 def cat(*a):
@@ -76,31 +79,30 @@
     a0, b0 = near(hid, "y")
     f0 = far(a0, b0, "y")
     za = after(za, a0, b0)
-    zf = far(za, zb, "zhi")
-    mid = cat(za, zb)
+    mid = after(cat(za, zb), f0)
     a1, b1 = near(mid, "y")
-    other = after(other, za, zb)
+    other = after(other, mid)
+    zf = far(after(za, other), zb, "zhi")
+    f1 = far(a1, b1, "y")
     pseudo = (chip_sum(zlo) + other.astype(f32)) * (1.0 / replicas)
     velocity = outer_mu * momentum + pseudo
     new = (outer_head.astype(f32) - outer_lr * (pseudo + outer_mu * velocity)).astype(bf16)
     xa, xb = near(new, "x")
-    f1 = far(a1, b1, "y")
-    a2, b2 = near(after(zf, a1, b1), "y")
     xf = far(xa, xb, "x")
-    f2 = far(a2, b2, "y")
+    zfx = zf
+    c1, c2 = near(zfx, "y")
 
-    def stack(own, lower, upper, ends):
-        n = own.shape[0] // replicas
-        buf = jnp.zeros((n, 4, replicas * tok, rows), bf16)
+    def put(buf, at, blk, dy):
+        n = blk.shape[0] // replicas
+        blk = blk.reshape(n, 1, replicas * tok, rows)
+        return lax.dynamic_update_slice(buf, blk, (at, (y + 4 + dy) % 4, 0, 0))
+
+    buf = jnp.zeros((3, 4, replicas * tok, rows), bf16)
+    for at, own, lower, upper, ends in ((0, hid, a0, b0, f0), (1, mid, a1, b1, f1)):
         for dy, blk in ((0, own), (-1, lower), (1, upper), (2, ends)):
-            blk = blk.reshape(n, 1, replicas * tok, rows)
-            buf = lax.dynamic_update_slice(buf, blk, (0, (y + dy) % 4, 0, 0))
-        return buf.reshape(n * 4 * replicas * tok, rows)
+            buf = put(buf, at, blk, dy)
+    lhs1 = buf.reshape(12 * replicas * tok, rows)
 
-    lhs1 = cat(stack(hid, a0, b0, f0), stack(mid, a1, b1, f1))
-    lhs2 = stack(zf, a2, b2, f2)
-
-    heads = [new, xa, xb, xf]
     away = (0, -1, 1, 2)
 
     want = lax.dynamic_slice_in_dim(targets[0], x * 16 * tok, 16 * tok, 0).reshape(4, 4, tok)
@@ -109,16 +111,23 @@
     want = jnp.stack([want[d % 4] for d in away]).reshape(16, tok)
     place = y * 4 + zhi
 
-    def reduce_part(units):
+    def partial(units, *deps):
         part = cat(*[
-            jnp.dot(lhs, heads[j], preferred_element_type=f32).reshape(-1, 2, 2, tok, width)
-            for _, lhs, j in units
+            jnp.dot(lhs, h, preferred_element_type=f32).reshape(-1, 2, 2, tok, width)
+            for _, lhs, _, h in units
         ])
-        both = lax.ppermute(pick(part, 1 - core, 2), "core", SWAP) + pick(part, core, 2)
-        rest = lax.ppermute(pick(both, 1 - zlo, 1), "zlo", SWAP)
+        half = pick(part, 1 - core, 2)
+        if deps:
+            half = after(half, *deps)
+        both = lax.ppermute(half, "core", SWAP) + pick(part, core, 2)
+        return both, pick(both, 1 - zlo, 1)
+
+    stats = {}
+
+    def finish(units, both, rest):
         logits = rest + pick(both, zlo, 1)
         at = 0
-        for g, lhs, j in units:
+        for g, lhs, j, _ in units:
             n = lhs.shape[0] // (replicas * tok)
             part = logits[at:at + n]
             at += n
@@ -129,10 +138,25 @@
             hit = jnp.sum(jnp.where(ids == want[g:g + n, :, None], part, 0.0), axis=2)
             stats[g, j] = jnp.stack([top, total, hit], axis=1)
 
-    stats = {}
-    reduce_part([(0, lhs1, 0)])
-    reduce_part([(0, lhs1, 1), (0, lhs1, 2)])
-    reduce_part([(0, lhs1, 3)] + [(12, lhs2, j) for j in range(4)])
+    u1 = [(0, lhs1, 0, new), (0, lhs1, 1, xa)]
+    both1, send1 = partial(u1)
+    rest1 = lax.ppermute(send1, "zlo", SWAP)
+    u2 = [(0, lhs1, 2, after(xb, send1))]
+    both2, send2 = partial(u2)
+    rest2 = lax.ppermute(after(send2, rest1), "zlo", SWAP)
+    c3 = far(c1, c2, "y")
+    buf = jnp.zeros((1, 4, replicas * tok, rows), bf16)
+    for dy, blk in ((0, zf), (-1, c1), (1, c2), (2, c3)):
+        buf = put(buf, 0, blk, dy)
+    lhs2 = buf.reshape(4 * replicas * tok, rows)
+    xf = after(xf, rest1)
+    u3 = [(0, lhs1, 3, xf)] + [(12, lhs2, j, h) for j, h in enumerate((new, xa, xb, xf))]
+    both3, send3 = partial(u3, rest2)
+    rest3 = lax.ppermute(after(send3, rest2), "zlo", SWAP)
+    finish(u1, both1, rest1)
+    finish(u2, both2, rest2)
+    finish(u3, both3, rest3)
+
     table = jnp.stack([cat(stats[0, j], stats[12, j]) for j in range(4)], axis=1)
     table = table.reshape(4, 4, 12 * tok)
     table = jnp.stack([table[away.index(d)] for d in (0, 1, 2, -1)])

time: 179 us -> 167 us (0.933)
  waiting for transfers between devices: 103 us -> 95 us
  starting transfers between devices: 29.2 us -> 26.9 us
  other arithmetic: 13.7 us -> 11.4 us
    ppermute x11, waiting for transfers between devices: 71.5 us -> 42.9 us  [the longest x1 16.3 us: shards(): rest3 = lax.ppermute(after(send3, rest2), 'zlo', SWAP)]
    ppermute x1, waiting for transfers between devices: 0.01 us -> 17.8 us  [shards(): other = lax.ppermute(send, 'zlo', SWAP)]
    ppermute x10, waiting for transfers between devices: 26.8 us -> 30.6 us  [shift(): return lax.ppermute(a, axis, [(i, (i + by) % n) for i in range(n)])]
    ppermute x11, starting transfers between devices: 6.96 us -> 4.6 us  [the longest x5 3.14 us: onward(): return lax.ppermute(a, ('core', axis), up + down)]
    add x7, other arithmetic: 4.75 us -> 2.46 us  [the longest x3 2.26 us: partial(): both = lax.ppermute(half, 'core', SWAP) + pick(part, core, 2)]
    unnamed x29 -> x27, local copies, waits for them, and re-layouts: 0.21 us -> 2.17 us
  transfers between devices with their start and end apart: 25 -> 25, of which waited for: 13 -> 13; matrix products, arithmetic and copies ran while one was open for 13% -> 11% of each run, Pallas kernels for 0% -> 0%
where the time goes in v3:
time: 167 us; the launch traced here: 165 us
  waiting for transfers between devices  95 us (57%)
  starting transfers between devices  26.9 us (16%)
  blocking collectives  14.6 us (9%)
  other arithmetic  11.4 us (7%)
  matrix products  8.47 us (5%)
  local copies, waits for them, and re-layouts  7.67 us (5%)
    ppermute x10, waiting for transfers between devices, shift(): return lax.ppermute(a, axis, [(i, (i + by) % n) for i in range(n)])  30.6 us
    ppermute x10, starting transfers between devices, shift(): return lax.ppermute(a, axis, [(i, (i + by) % n) for i in range(n)])  17.8 us
    ppermute x1, waiting for transfers between devices, shards(): other = lax.ppermute(send, 'zlo', SWAP)  17.8 us
    ppermute x1, waiting for transfers between devices, shards(): rest3 = lax.ppermute(after(send3, rest2), 'zlo', SWAP)  16.3 us
    all_to_all x1, blocking collectives, shards(): lax.all_to_all(table.reshape(16, 12 * tok), ('zhi', 'y'), 0, 0, tiled=True)  14.6 us
    ppermute x1, waiting for transfers between devices, shards(): rest1 = lax.ppermute(send1, 'zlo', SWAP)  11.1 us
    ppermute x5, waiting for transfers between devices, onward(): return lax.ppermute(a, ('core', axis), up + down)  8.96 us
    dot_general x8, matrix products, partial(): jnp.dot(lhs, h, preferred_element_type=f32).reshape(-1, 2, 2, tok, width)  8.47 us
  transfers between devices with their start and end apart: 25, of which 13 were waited for; matrix products, arithmetic and copies ran while one was open for 11% of the time, Pallas kernels for 0%

profile of v3, /device:TPU:0, one launch (start us, length us, event | category | flops | bytes accessed | tf_op | source)
XLA Modules:
  0.0 165.0 jit_solution(1012191509604232695)
XLA Ops:
  0.0 1.8 %dynamic-slice_bitcast_fusion = bf16[2,2048,256]{2,1,0:T(8,128)(2,1)S(1)} fusion(bf16[2,2,2048,256]{3,2,1,0:T(8,128)(2,1)} %bitcast.171, s32[]{:T(128)S(6)} %select_n.202), kind=kLoop, calls=%fused_computation.14 | loop fusion | bytes 4194308 | tf_op jit(solution)/shard_map/jit(dynamic_index_in_dim)/squeeze | solution.py:16
  2.2 1.0 copy.40
  3.2 3.5 %all-to-all-start = ((bf16[4,24,2048]{2,1,0:T(8,128)(2,1)}), bf16[4,24,2048]{2,1,0:T(8,128)(2,1)S(1)}, u32[]{:S(2)}, u32[]{:S(2)}) async-start(bf16[4,24,2048]{2,1,0:T(8,128)(2,1)} %copy.40), calls=%async_computation | async-start | bytes 786432 | tf_op jit(solution)/shard_map/all_to_all | solution.py:67
  8.7 1.9 %fusion.4 = bf16[2048,256]{1,0:T(8,128)(2,1)S(1)} fusion(f32[16,256]{1,0:T(8,128)S(1)} %get-tuple-element.61, bf16[2,2048,256]{2,1,0:T(8,128)(2,1)} %collective-permute-done, s32[]{:T(128)S(6)} %select_n.198, f32[16,256]{1,0:T(8,128)S(1)} %get-tuple-element.59, bf16[2,2,2048,256]{3,2,1,0:T(8,128)(2,1)} %bitcast.172, s32[]{:T(128)S(6)} %select_n.199, ...), kind=kLoop, calls=%fused_computation.11 | loop fusion | flops 3145728 | bytes 3178508 | tf_op jit(solution)/shard_map/convert_element_type | solution.py:75
  10.6 3.4 %all-to-all-done = bf16[4,24,2048]{2,1,0:T(8,128)(2,1)S(1)} async-done(((bf16[4,24,2048]{2,1,0:T(8,128)(2,1)}), bf16[4,24,2048]{2,1,0:T(8,128)(2,1)S(1)}, u32[]{:S(2)}, u32[]{:S(2)}) %all-to-all-start) | async-done | bytes 393248 | tf_op jit(solution)/shard_map/all_to_all | solution.py:67
  14.1 3.2 %collective-permute-start.3 = (bf16[4,24,2048]{2,1,0:T(8,128)(2,1)S(1)}, bf16[4,24,2048]{2,1,0:T(8,128)(2,1)S(1)}, u32[]{:S(2)}, u32[]{:S(2)}) collective-permute-start(bf16[4,24,2048]{2,1,0:T(8,128)(2,1)S(1)} %all-to-all-done), channel_id=1, source_target_pairs={{0,12},{4,0},{8,4},{12,8},{1,13},{5,1},{9,5},{13,9},{2,14},{6,2},{... | collective-permute-start | bytes 1179656 | tf_op jit(solution)/shard_map/ppermute | solution.py:21
  17.3 1.8 %collective-permute-start.5 = (bf16[4,24,2048]{2,1,0:T(8,128)(2,1)S(1)}, bf16[4,24,2048]{2,1,0:T(8,128)(2,1)S(1)}, u32[]{:S(2)}, u32[]{:S(2)}) collective-permute-start(bf16[4,24,2048]{2,1,0:T(8,128)(2,1)S(1)} %all-to-all-done), channel_id=1, source_target_pairs={{0,1},{1,2},{2,3},{3,0},{4,5},{5,6},{6,7},{7,4},{8,9},{9,10},{10,1... | collective-permute-start | bytes 1179656 | tf_op jit(solution)/shard_map/ppermute | solution.py:21
  19.1 2.8 %collective-permute-start.6 = (bf16[4,24,2048]{2,1,0:T(8,128)(2,1)S(1)}, bf16[4,24,2048]{2,1,0:T(8,128)(2,1)S(1)}, u32[]{:S(2)}, u32[]{:S(2)}) collective-permute-start(bf16[4,24,2048]{2,1,0:T(8,128)(2,1)S(1)} %all-to-all-done), channel_id=1, source_target_pairs={{0,3},{1,0},{2,1},{3,2},{4,7},{5,4},{6,5},{7,6},{8,11},{9,8},{10,9... | collective-permute-start | bytes 1179656 | tf_op jit(solution)/shard_map/ppermute | solution.py:21
  22.2 3.7 %collective-permute-done.2 = bf16[4,24,2048]{2,1,0:T(8,128)(2,1)S(1)} collective-permute-done((bf16[4,24,2048]{2,1,0:T(8,128)(2,1)S(1)}, bf16[4,24,2048]{2,1,0:T(8,128)(2,1)S(1)}, u32[]{:S(2)}, u32[]{:S(2)}) %collective-permute-start.2) | collective-permute-done | bytes 393248 | tf_op jit(solution)/shard_map/ppermute | solution.py:21
  27.0 13.2 %collective-permute-done.5 = bf16[4,24,2048]{2,1,0:T(8,128)(2,1)S(1)} collective-permute-done((bf16[4,24,2048]{2,1,0:T(8,128)(2,1)S(1)}, bf16[4,24,2048]{2,1,0:T(8,128)(2,1)S(1)}, u32[]{:S(2)}, u32[]{:S(2)}) %collective-permute-start.5) | collective-permute-done | bytes 393248 | tf_op jit(solution)/shard_map/ppermute | solution.py:21
  40.7 2.9 %collective-permute-start.8 = (bf16[8,24,2048]{2,1,0:T(8,128)(2,1)S(1)}, bf16[8,24,2048]{2,1,0:T(8,128)(2,1)S(1)}, u32[]{:S(2)}, u32[]{:S(2)}) collective-permute-start(bf16[8,24,2048]{2,1,0:T(8,128)(2,1)S(1)} %pad_maximum_fusion), channel_id=1, source_target_pairs={{0,12},{4,0},{8,4},{12,8},{1,13},{5,1},{9,5},{13,9},{2,14},{6,2},{... | collective-permute-start | bytes 2359304 | tf_op jit(solution)/shard_map/ppermute | solution.py:21
  43.7 17.8 %collective-permute-done.10 = bf16[2048,256]{1,0:T(8,128)(2,1)S(1)} collective-permute-done((bf16[2048,256]{1,0:T(8,128)(2,1)S(1)}, bf16[2048,256]{1,0:T(8,128)(2,1)S(1)}, u32[]{:S(2)}, u32[]{:S(2)}) %collective-permute-start.10) | collective-permute-done | bytes 1048608 | tf_op jit(solution)/shard_map/ppermute | solution.py:77
  61.6 1.6 collective-permute-start.16
  63.8 2.7 %subtract_convert_fusion = bf16[2048,256]{1,0:T(8,128)(2,1)S(1)} fusion(f32[2048,256]{1,0:T(8,128)S(1)} %copy-done.2, bf16[2048,256]{1,0:T(8,128)(2,1)S(1)} %collective-permute-done.10, bf16[2048,256]{1,0:T(8,128)(2,1)S(1)} %copy-done.3, f32[16,256]{1,0:T(8,128)S(1)} %copy-done.8, bf16[2,2048,256]{2,1,0:T(8,128)(2,1)} %collective-permute-done, ...), kind=kLoop, calls=%fused_computation.13 | loop fusion | flops 8388608 | bytes 7372812 | tf_op jit(solution)/shard_map/convert_element_type | solution.py:89
  66.5 1.7 %collective-permute-start.11 = (bf16[2048,256]{1,0:T(8,128)(2,1)S(1)}, bf16[2048,256]{1,0:T(8,128)(2,1)S(1)}, u32[]{:S(2)}, u32[]{:S(2)}) collective-permute-start(bf16[2048,256]{1,0:T(8,128)(2,1)S(1)} %subtract_convert_fusion), channel_id=1, source_target_pairs={{0,16},{16,32},{32,48},{48,0},{1,17},{17,33},{33,49},{49,1},{2,18}... | collective-permute-start | bytes 3145736 | tf_op jit(solution)/shard_map/ppermute | solution.py:21
  68.3 1.7 %collective-permute-start.14 = (bf16[2048,256]{1,0:T(8,128)(2,1)S(1)}, bf16[2048,256]{1,0:T(8,128)(2,1)S(1)}, u32[]{:S(2)}, u32[]{:S(2)}) collective-permute-start(bf16[2048,256]{1,0:T(8,128)(2,1)S(1)} %subtract_convert_fusion), channel_id=1, source_target_pairs={{0,48},{16,0},{32,16},{48,32},{1,49},{17,1},{33,17},{49,33},{2,50}... | collective-permute-start | bytes 3145736 | tf_op jit(solution)/shard_map/ppermute | solution.py:21
  70.0 4.7 %collective-permute-done.16 = bf16[4,24,2048]{2,1,0:T(8,128)(2,1)S(1)} collective-permute-done((bf16[4,24,2048]{2,1,0:T(8,128)(2,1)S(1)}, bf16[4,24,2048]{2,1,0:T(8,128)(2,1)S(1)}, u32[]{:S(2)}, u32[]{:S(2)}) %collective-permute-start.16) | collective-permute-done | bytes 393248 | tf_op jit(solution)/shard_map/ppermute | solution.py:39
  75.0 2.9 %collective-permute-start.18 = (bf16[4,24,2048]{2,1,0:T(8,128)(2,1)S(1)}, bf16[4,24,2048]{2,1,0:T(8,128)(2,1)S(1)}, u32[]{:S(2)}, u32[]{:S(2)}) collective-permute-start(bf16[4,24,2048]{2,1,0:T(8,128)(2,1)S(1)} %collective-permute-done.16), channel_id=1, source_target_pairs={{0,12},{4,0},{8,4},{12,8},{1,13},{5,1},{9,5},{13,9},{2,14},{6,2},{... | collective-permute-start | bytes 1179656 | tf_op jit(solution)/shard_map/ppermute | solution.py:21
  78.2 1.5 fusion.19
  79.7 13.7 %collective-permute-done.11 = bf16[2048,256]{1,0:T(8,128)(2,1)S(1)} collective-permute-done((bf16[2048,256]{1,0:T(8,128)(2,1)S(1)}, bf16[2048,256]{1,0:T(8,128)(2,1)S(1)}, u32[]{:S(2)}, u32[]{:S(2)}) %collective-permute-start.11) | collective-permute-done | bytes 1048608 | tf_op jit(solution)/shard_map/ppermute | solution.py:21
  93.4 1.5 fusion.16
  96.3 1.6 collective-permute-done.12
  98.2 1.5 fusion.10
  100.2 4.2 %collective-permute-done.19 = bf16[4,24,2048]{2,1,0:T(8,128)(2,1)S(1)} collective-permute-done((bf16[4,24,2048]{2,1,0:T(8,128)(2,1)S(1)}, bf16[4,24,2048]{2,1,0:T(8,128)(2,1)S(1)}, u32[]{:S(2)}, u32[]{:S(2)}) %collective-permute-start.19) | collective-permute-done | bytes 393248 | tf_op jit(solution)/shard_map/ppermute | solution.py:39
  104.7 11.1 %collective-permute-done.13 = f32[24,24,256]{2,1,0:T(8,128)S(1)} collective-permute-done((f32[24,24,256]{2,1,0:T(8,128)S(1)}, f32[24,24,256]{2,1,0:T(8,128)S(1)}, u32[]{:S(2)}, u32[]{:S(2)}) %collective-permute-start.13) | collective-permute-done | bytes 589856 | tf_op jit(solution)/shard_map/ppermute | solution.py:143
  116.6 1.5 convolution_dynamic-update-slice_fusion
  120.6 1.5 copy-done.1
  122.3 1.9 %collective-permute-done.21 = f32[12,24,256]{2,1,0:T(8,128)S(1)} collective-permute-done((f32[12,24,256]{2,1,0:T(8,128)S(1)}, f32[12,24,256]{2,1,0:T(8,128)S(1)}, u32[]{:S(2)}, u32[]{:S(2)}) %collective-permute-start.21) | collective-permute-done | bytes 294944 | tf_op jit(solution)/shard_map/ppermute | solution.py:146
  124.5 3.0 %collective-permute-done.22 = f32[28,2,24,256]{3,2,1,0:T(8,128)} collective-permute-done((f32[28,2,24,256]{3,2,1,0:T(8,128)S(1)}, f32[28,2,24,256]{3,2,1,0:T(8,128)}, u32[]{:S(2)}, u32[]{:S(2)}) %collective-permute-start.22) | collective-permute-done | bytes 1376288 | tf_op jit(solution)/shard_map/ppermute | solution.py:122
  127.5 2.0 %bitcast_add_fusion = f32[28,2,24,256]{3,2,1,0:T(8,128)S(1)} fusion(f32[28,2,24,256]{3,2,1,0:T(8,128)} %collective-permute-done.22, f32[28,2,2,24,256]{4,3,2,1,0:T(8,128)} %copy-done.1, s32[]{:T(128)S(6)} %select_n.200), kind=kLoop, calls=%fused_computation.16 | loop fusion | flops 344064 | bytes 4128772 | tf_op jit(solution)/shard_map/add | solution.py:122
  130.8 16.3 %collective-permute-done.23 = f32[28,24,256]{2,1,0:T(8,128)S(1)} collective-permute-done((f32[28,24,256]{2,1,0:T(8,128)S(1)}, f32[28,24,256]{2,1,0:T(8,128)S(1)}, u32[]{:S(2)}, u32[]{:S(2)}) %collective-permute-start.23) | collective-permute-done | bytes 688160 | tf_op jit(solution)/shard_map/ppermute | solution.py:155
  149.4 14.6 %all_to_all.14 = f32[16,1,288]{2,1,0:T(1,128)S(1)} all-to-all(f32[16,1,288]{2,1,0:T(1,128)S(1)} %all_to_all.10), channel_id=1, replica_groups=mesh['zlo'=2,'core'=2,'x'=4,'y'=4,'zhi'=4] {'zhi','y'}, dimensions={0} | all-to-all | bytes 36864 | tf_op jit(solution)/shard_map/all_to_all | solution.py:164
  (150 shorter events, 15.7 us)
Async XLA Ops:
  0.0 124.2 %copy-start = (s32[1,1536]{1,0:T(1,128)S(1)}, s32[1,1536]{1,0:T(1,128)}, u32[]{:S(2)}) copy-start(s32[1,1536]{1,0:T(1,128)} %param.11) | copy-start | bytes 18436
  1.8 4.9 %copy-start.9 = (bf16[1,64,256]{2,1,0:T(8,128)(2,1)S(1)}, bf16[1,64,256]{2,1,0:T(8,128)(2,1)}, u32[]{:S(2)}) copy-start(bf16[1,64,256]{2,1,0:T(8,128)(2,1)} %param.7) | copy-start | bytes 98308
  1.8 6.9 %collective-permute-start = (bf16[2,2048,256]{2,1,0:T(8,128)(2,1)S(1)}, bf16[2,2048,256]{2,1,0:T(8,128)(2,1)}, u32[]{:S(2)}, u32[]{:S(2)}) collective-permute-start(bf16[2,2048,256]{2,1,0:T(8,128)(2,1)S(1)} %dynamic-slice_bitcast_fusion), channel_id=1, source_target_pairs={{0,64},{64,0},{1,65},{65,1},{2,66},{66,2},{3,67},{67,3},{4,68},{68... | collective-permute-start | bytes 6291464 | tf_op jit(solution)/shard_map/ppermute | solution.py:61
  3.2 10.9 %all-to-all-start = ((bf16[4,24,2048]{2,1,0:T(8,128)(2,1)}), bf16[4,24,2048]{2,1,0:T(8,128)(2,1)S(1)}, u32[]{:S(2)}, u32[]{:S(2)}) async-start(bf16[4,24,2048]{2,1,0:T(8,128)(2,1)} %copy.40), calls=%async_computation | async-start | bytes 786432 | tf_op jit(solution)/shard_map/all_to_all | solution.py:67
  6.7 1.4 collective-permute-start.1
  14.1 11.9 %collective-permute-start.2 = (bf16[4,24,2048]{2,1,0:T(8,128)(2,1)S(1)}, bf16[4,24,2048]{2,1,0:T(8,128)(2,1)S(1)}, u32[]{:S(2)}, u32[]{:S(2)}) collective-permute-start(bf16[4,24,2048]{2,1,0:T(8,128)(2,1)S(1)} %all-to-all-done), channel_id=1, source_target_pairs={{0,4},{4,8},{8,12},{12,0},{1,5},{5,9},{9,13},{13,1},{2,6},{6,10},{... | collective-permute-start | bytes 1179656 | tf_op jit(solution)/shard_map/ppermute | solution.py:21
  14.1 11.8 %collective-permute-start.3 = (bf16[4,24,2048]{2,1,0:T(8,128)(2,1)S(1)}, bf16[4,24,2048]{2,1,0:T(8,128)(2,1)S(1)}, u32[]{:S(2)}, u32[]{:S(2)}) collective-permute-start(bf16[4,24,2048]{2,1,0:T(8,128)(2,1)S(1)} %all-to-all-done), channel_id=1, source_target_pairs={{0,12},{4,0},{8,4},{12,8},{1,13},{5,1},{9,5},{13,9},{2,14},{6,2},{... | collective-permute-start | bytes 1179656 | tf_op jit(solution)/shard_map/ppermute | solution.py:21
  17.3 22.9 %collective-permute-start.5 = (bf16[4,24,2048]{2,1,0:T(8,128)(2,1)S(1)}, bf16[4,24,2048]{2,1,0:T(8,128)(2,1)S(1)}, u32[]{:S(2)}, u32[]{:S(2)}) collective-permute-start(bf16[4,24,2048]{2,1,0:T(8,128)(2,1)S(1)} %all-to-all-done), channel_id=1, source_target_pairs={{0,1},{1,2},{2,3},{3,0},{4,5},{5,6},{6,7},{7,4},{8,9},{9,10},{10,1... | collective-permute-start | bytes 1179656 | tf_op jit(solution)/shard_map/ppermute | solution.py:21
  19.1 21.1 %collective-permute-start.6 = (bf16[4,24,2048]{2,1,0:T(8,128)(2,1)S(1)}, bf16[4,24,2048]{2,1,0:T(8,128)(2,1)S(1)}, u32[]{:S(2)}, u32[]{:S(2)}) collective-permute-start(bf16[4,24,2048]{2,1,0:T(8,128)(2,1)S(1)} %all-to-all-done), channel_id=1, source_target_pairs={{0,3},{1,0},{2,1},{3,2},{4,7},{5,4},{6,5},{7,6},{8,11},{9,8},{10,9... | collective-permute-start | bytes 1179656 | tf_op jit(solution)/shard_map/ppermute | solution.py:21
  21.9 39.7 %collective-permute-start.10 = (bf16[2048,256]{1,0:T(8,128)(2,1)S(1)}, bf16[2048,256]{1,0:T(8,128)(2,1)S(1)}, u32[]{:S(2)}, u32[]{:S(2)}) collective-permute-start(bf16[2048,256]{1,0:T(8,128)(2,1)S(1)} %fusion.4), channel_id=1, source_target_pairs={{0,128},{128,0},{1,129},{129,1},{2,130},{130,2},{3,131},{131,3},{4... | collective-permute-start | bytes 3145736 | tf_op jit(solution)/shard_map/ppermute | solution.py:77
  26.0 14.3 %collective-permute-start.4 = (bf16[4,24,2048]{2,1,0:T(8,128)(2,1)S(1)}, bf16[4,24,2048]{2,1,0:T(8,128)(2,1)S(1)}, u32[]{:S(2)}, u32[]{:S(2)}) collective-permute-start(bf16[4,24,2048]{2,1,0:T(8,128)(2,1)S(1)} %broadcast_select_fusion.4), channel_id=1, source_target_pairs={{0,4},{4,8},{8,12},{12,0},{68,64},{72,68},{76,72},{64,76},{1,5},{5... | collective-permute-start | bytes 1179656 | tf_op jit(solution)/shard_map/ppermute | solution.py:39
  40.3 22.9 %collective-permute-start.7 = (bf16[8,24,2048]{2,1,0:T(8,128)(2,1)S(1)}, bf16[8,24,2048]{2,1,0:T(8,128)(2,1)S(1)}, u32[]{:S(2)}, u32[]{:S(2)}) collective-permute-start(bf16[8,24,2048]{2,1,0:T(8,128)(2,1)S(1)} %pad_maximum_fusion), channel_id=1, source_target_pairs={{0,4},{4,8},{8,12},{12,0},{1,5},{5,9},{9,13},{13,1},{2,6},{6,10},{... | collective-permute-start | bytes 2359304 | tf_op jit(solution)/shard_map/ppermute | solution.py:21
  40.7 22.5 %collective-permute-start.8 = (bf16[8,24,2048]{2,1,0:T(8,128)(2,1)S(1)}, bf16[8,24,2048]{2,1,0:T(8,128)(2,1)S(1)}, u32[]{:S(2)}, u32[]{:S(2)}) collective-permute-start(bf16[8,24,2048]{2,1,0:T(8,128)(2,1)S(1)} %pad_maximum_fusion), channel_id=1, source_target_pairs={{0,12},{4,0},{8,4},{12,8},{1,13},{5,1},{9,5},{13,9},{2,14},{6,2},{... | collective-permute-start | bytes 2359304 | tf_op jit(solution)/shard_map/ppermute | solution.py:21
  61.6 2.2 %copy-start.2 = (f32[2048,256]{1,0:T(8,128)S(1)}, f32[2048,256]{1,0:T(8,128)}, u32[]{:S(2)}) copy-start(f32[2048,256]{1,0:T(8,128)} %param.9) | copy-start | bytes 6291460
  61.6 2.2 %copy-start.3 = (bf16[2048,256]{1,0:T(8,128)(2,1)S(1)}, bf16[2048,256]{1,0:T(8,128)(2,1)}, u32[]{:S(2)}) copy-start(bf16[2048,256]{1,0:T(8,128)(2,1)} %param.8) | copy-start | bytes 3145732
  61.6 2.2 %copy-start.7 = (f32[16,256]{1,0:T(8,128)S(1)}, f32[16,256]{1,0:T(8,128)}, u32[]{:S(2)}) copy-start(f32[16,256]{1,0:T(8,128)} %get-tuple-element.58) | copy-start | bytes 49156
  61.6 2.2 %copy-start.8 = (f32[16,256]{1,0:T(8,128)S(1)}, f32[16,256]{1,0:T(8,128)}, u32[]{:S(2)}) copy-start(f32[16,256]{1,0:T(8,128)} %get-tuple-element.60) | copy-start | bytes 49156
  61.6 13.1 %collective-permute-start.16 = (bf16[4,24,2048]{2,1,0:T(8,128)(2,1)S(1)}, bf16[4,24,2048]{2,1,0:T(8,128)(2,1)S(1)}, u32[]{:S(2)}, u32[]{:S(2)}) collective-permute-start(bf16[4,24,2048]{2,1,0:T(8,128)(2,1)S(1)} %broadcast_select_fusion.3), channel_id=1, source_target_pairs={{0,1},{1,2},{2,3},{3,0},{65,64},{66,65},{67,66},{64,67},{4,5},{5,6... | collective-permute-start | bytes 1179656 | tf_op jit(solution)/shard_map/ppermute | solution.py:39
  63.3 14.9 %collective-permute-start.9 = (bf16[8,24,2048]{2,1,0:T(8,128)(2,1)S(1)}, bf16[8,24,2048]{2,1,0:T(8,128)(2,1)S(1)}, u32[]{:S(2)}, u32[]{:S(2)}) collective-permute-start(bf16[8,24,2048]{2,1,0:T(8,128)(2,1)S(1)} %broadcast_select_fusion.1), channel_id=1, source_target_pairs={{0,4},{4,8},{8,12},{12,0},{68,64},{72,68},{76,72},{64,76},{1,5},{5... | collective-permute-start | bytes 2359304 | tf_op jit(solution)/shard_map/ppermute | solution.py:39
  66.5 26.9 %collective-permute-start.11 = (bf16[2048,256]{1,0:T(8,128)(2,1)S(1)}, bf16[2048,256]{1,0:T(8,128)(2,1)S(1)}, u32[]{:S(2)}, u32[]{:S(2)}) collective-permute-start(bf16[2048,256]{1,0:T(8,128)(2,1)S(1)} %subtract_convert_fusion), channel_id=1, source_target_pairs={{0,16},{16,32},{32,48},{48,0},{1,17},{17,33},{33,49},{49,1},{2,18}... | collective-permute-start | bytes 3145736 | tf_op jit(solution)/shard_map/ppermute | solution.py:21
  68.3 27.6 %collective-permute-start.14 = (bf16[2048,256]{1,0:T(8,128)(2,1)S(1)}, bf16[2048,256]{1,0:T(8,128)(2,1)S(1)}, u32[]{:S(2)}, u32[]{:S(2)}) collective-permute-start(bf16[2048,256]{1,0:T(8,128)(2,1)S(1)} %subtract_convert_fusion), channel_id=1, source_target_pairs={{0,48},{16,0},{32,16},{48,32},{1,49},{17,1},{33,17},{49,33},{2,50}... | collective-permute-start | bytes 3145736 | tf_op jit(solution)/shard_map/ppermute | solution.py:21
  74.7 20.6 %collective-permute-start.17 = (bf16[4,24,2048]{2,1,0:T(8,128)(2,1)S(1)}, bf16[4,24,2048]{2,1,0:T(8,128)(2,1)S(1)}, u32[]{:S(2)}, u32[]{:S(2)}) collective-permute-start(bf16[4,24,2048]{2,1,0:T(8,128)(2,1)S(1)} %collective-permute-done.16), channel_id=1, source_target_pairs={{0,4},{4,8},{8,12},{12,0},{1,5},{5,9},{9,13},{13,1},{2,6},{6,10},{... | collective-permute-start | bytes 1179656 | tf_op jit(solution)/shard_map/ppermute | solution.py:21
  75.0 20.3 %collective-permute-start.18 = (bf16[4,24,2048]{2,1,0:T(8,128)(2,1)S(1)}, bf16[4,24,2048]{2,1,0:T(8,128)(2,1)S(1)}, u32[]{:S(2)}, u32[]{:S(2)}) collective-permute-start(bf16[4,24,2048]{2,1,0:T(8,128)(2,1)S(1)} %collective-permute-done.16), channel_id=1, source_target_pairs={{0,12},{4,0},{8,4},{12,8},{1,13},{5,1},{9,5},{13,9},{2,14},{6,2},{... | collective-permute-start | bytes 1179656 | tf_op jit(solution)/shard_map/ppermute | solution.py:21
  95.0 2.9 %collective-permute-start.12 = (f32[24,2,24,256]{3,2,1,0:T(8,128)S(1)}, f32[24,2,24,256]{3,2,1,0:T(8,128)S(1)}, u32[]{:S(2)}, u32[]{:S(2)}) collective-permute-start(f32[24,2,24,256]{3,2,1,0:T(8,128)S(1)} %fusion.9), channel_id=1, source_target_pairs={{0,64},{64,0},{1,65},{65,1},{2,66},{66,2},{3,67},{67,3},{4,68},{68... | collective-permute-start | bytes 3538952 | tf_op jit(solution)/shard_map/ppermute | solution.py:122
  95.4 9.1 %collective-permute-start.19 = (bf16[4,24,2048]{2,1,0:T(8,128)(2,1)S(1)}, bf16[4,24,2048]{2,1,0:T(8,128)(2,1)S(1)}, u32[]{:S(2)}, u32[]{:S(2)}) collective-permute-start(bf16[4,24,2048]{2,1,0:T(8,128)(2,1)S(1)} %broadcast_select_fusion.2), channel_id=1, source_target_pairs={{0,4},{4,8},{8,12},{12,0},{68,64},{72,68},{76,72},{64,76},{1,5},{5... | collective-permute-start | bytes 1179656 | tf_op jit(solution)/shard_map/ppermute | solution.py:39
  96.0 20.6 %collective-permute-start.15 = (bf16[2048,256]{1,0:T(8,128)(2,1)S(1)}, bf16[2048,256]{1,0:T(8,128)(2,1)S(1)}, u32[]{:S(2)}, u32[]{:S(2)}) collective-permute-start(bf16[2048,256]{1,0:T(8,128)(2,1)S(1)} %broadcast_select_fusion), channel_id=1, source_target_pairs={{0,16},{16,32},{32,48},{48,0},{80,64},{96,80},{112,96},{64,112},{1... | collective-permute-start | bytes 3145736 | tf_op jit(solution)/shard_map/ppermute | solution.py:39
  99.8 4.8 %collective-permute-start.20 = (f32[12,2,24,256]{3,2,1,0:T(8,128)S(1)}, f32[12,2,24,256]{3,2,1,0:T(8,128)S(1)}, u32[]{:S(2)}, u32[]{:S(2)}) collective-permute-start(f32[12,2,24,256]{3,2,1,0:T(8,128)S(1)} %dynamic-slice_bitcast_fusion.3), channel_id=1, source_target_pairs={{0,64},{64,0},{1,65},{65,1},{2,66},{66,2},{3,67},{67,3},{4,68},{68... | collective-permute-start | bytes 1769480 | tf_op jit(solution)/shard_map/ppermute | solution.py:122
  100.1 15.6 %collective-permute-start.13 = (f32[24,24,256]{2,1,0:T(8,128)S(1)}, f32[24,24,256]{2,1,0:T(8,128)S(1)}, u32[]{:S(2)}, u32[]{:S(2)}) collective-permute-start(f32[24,24,256]{2,1,0:T(8,128)S(1)} %dynamic-slice_bitcast_fusion.4), channel_id=1, source_target_pairs={{0,128},{128,0},{1,129},{129,1},{2,130},{130,2},{3,131},{131,3},{4... | collective-permute-start | bytes 1769480 | tf_op jit(solution)/shard_map/ppermute | solution.py:143
  115.8 8.4 %collective-permute-start.21 = (f32[12,24,256]{2,1,0:T(8,128)S(1)}, f32[12,24,256]{2,1,0:T(8,128)S(1)}, u32[]{:S(2)}, u32[]{:S(2)}) collective-permute-start(f32[12,24,256]{2,1,0:T(8,128)S(1)} %dynamic-slice_bitcast_fusion.5), channel_id=1, source_target_pairs={{0,128},{128,0},{1,129},{129,1},{2,130},{130,2},{3,131},{131,3},{4... | collective-permute-start | bytes 884744 | tf_op jit(solution)/shard_map/ppermute | solution.py:146
  124.2 3.3 %collective-permute-start.22 = (f32[28,2,24,256]{3,2,1,0:T(8,128)S(1)}, f32[28,2,24,256]{3,2,1,0:T(8,128)}, u32[]{:S(2)}, u32[]{:S(2)}) collective-permute-start(f32[28,2,24,256]{3,2,1,0:T(8,128)S(1)} %dynamic-slice_bitcast_fusion.1), channel_id=1, source_target_pairs={{0,64},{64,0},{1,65},{65,1},{2,66},{66,2},{3,67},{67,3},{4,68},{68... | collective-permute-start | bytes 4128776 | tf_op jit(solution)/shard_map/ppermute | solution.py:122
  124.5 5.7 %copy-start.5 = (f32[24,24,256]{2,1,0:T(8,128)S(1)}, f32[24,24,256]{2,1,0:T(8,128)}, u32[]{:S(2)}) copy-start(f32[24,24,256]{2,1,0:T(8,128)} %copy-done.4) | copy-start | bytes 1769476
  129.5 17.6 %collective-permute-start.23 = (f32[28,24,256]{2,1,0:T(8,128)S(1)}, f32[28,24,256]{2,1,0:T(8,128)S(1)}, u32[]{:S(2)}, u32[]{:S(2)}) collective-permute-start(f32[28,24,256]{2,1,0:T(8,128)S(1)} %dynamic-slice_bitcast_fusion.2), channel_id=1, source_target_pairs={{0,128},{128,0},{1,129},{129,1},{2,130},{130,2},{3,131},{131,3},{4... | collective-permute-start | bytes 2064392 | tf_op jit(solution)/shard_map/ppermute | solution.py:155
  (3 other events, 4.3 us)

commit v4 on v3

--- a/solution.py
+++ b/solution.py
@@ -158,11 +158,13 @@
     finish(u3, both3, rest3)
 
     table = jnp.stack([cat(stats[0, j], stats[12, j]) for j in range(4)], axis=1)
-    table = table.reshape(4, 4, 12 * tok)
+    top = jnp.max(table[:, :, 0], axis=1)
+    total = jnp.sum(table[:, :, 1] * jnp.exp(table[:, :, 0] - top[:, None]), axis=1)
+    table = jnp.concatenate([top, total, jnp.sum(table[:, :, 2], axis=1)], axis=1).reshape(4, 4, 3 * tok)
     table = jnp.stack([table[away.index(d)] for d in (0, 1, 2, -1)])
     table = lax.dynamic_slice_in_dim(cat(table, table), (4 - zhi) % 4, 4, 0)
-    table = lax.all_to_all(table.reshape(16, 12 * tok), ("zhi", "y"), 0, 0, tiled=True)
-    table = table.reshape(64, 3, tok)
+    table = lax.all_to_all(table.reshape(16, 3 * tok), ("zhi", "y"), 0, 0, tiled=True)
+    table = table.reshape(16, 3, tok)
     top, total, hit = table[:, 0], table[:, 1], table[:, 2]
     high = jnp.max(top, axis=0)
     total = jnp.sum(total * jnp.exp(top - high), axis=0)

time: 167 us -> 168 us (level)
  no operation moved by 1% of the time
where the time goes in v4:
time: 168 us; the launch traced here: 165 us
  waiting for transfers between devices  95 us (57%)
  starting transfers between devices  26.9 us (16%)
  blocking collectives  14.6 us (9%)
  other arithmetic  12 us (7%)
  matrix products  8.47 us (5%)
  local copies, waits for them, and re-layouts  7.57 us (5%)
    ppermute x10, waiting for transfers between devices, shift(): return lax.ppermute(a, axis, [(i, (i + by) % n) for i in range(n)])  30.6 us
    ppermute x10, starting transfers between devices, shift(): return lax.ppermute(a, axis, [(i, (i + by) % n) for i in range(n)])  17.8 us
    ppermute x1, waiting for transfers between devices, shards(): other = lax.ppermute(send, 'zlo', SWAP)  17.8 us
    ppermute x1, waiting for transfers between devices, shards(): rest3 = lax.ppermute(after(send3, rest2), 'zlo', SWAP)  16.3 us
    all_to_all x1, blocking collectives, shards(): lax.all_to_all(table.reshape(16, 3 * tok), ('zhi', 'y'), 0, 0, tiled=True)  14.6 us
    ppermute x1, waiting for transfers between devices, shards(): rest1 = lax.ppermute(send1, 'zlo', SWAP)  11.1 us
    ppermute x5, waiting for transfers between devices, onward(): return lax.ppermute(a, ('core', axis), up + down)  8.96 us
    dot_general x8, matrix products, partial(): jnp.dot(lhs, h, preferred_element_type=f32).reshape(-1, 2, 2, tok, width)  8.47 us
  transfers between devices with their start and end apart: 25, of which 13 were waited for; matrix products, arithmetic and copies ran while one was open for 11% of the time, Pallas kernels for 0%

profile of v4, /device:TPU:0, one launch (start us, length us, event | category | flops | bytes accessed | tf_op | source)
XLA Modules:
  0.0 165.2 jit_solution(7420041191403572444)
XLA Ops:
  0.0 1.8 %dynamic-slice_bitcast_fusion = bf16[2,2048,256]{2,1,0:T(8,128)(2,1)S(1)} fusion(bf16[2,2,2048,256]{3,2,1,0:T(8,128)(2,1)} %bitcast.223, s32[]{:T(128)S(6)} %select_n.202), kind=kLoop, calls=%fused_computation.14 | loop fusion | bytes 4194308 | tf_op jit(solution)/shard_map/jit(dynamic_index_in_dim)/squeeze | solution.py:16
  2.2 1.0 copy.35
  3.2 3.5 %all-to-all-start = ((bf16[4,24,2048]{2,1,0:T(8,128)(2,1)}), bf16[4,24,2048]{2,1,0:T(8,128)(2,1)S(1)}, u32[]{:S(2)}, u32[]{:S(2)}) async-start(bf16[4,24,2048]{2,1,0:T(8,128)(2,1)} %copy.35), calls=%async_computation | async-start | bytes 786432 | tf_op jit(solution)/shard_map/all_to_all | solution.py:67
  8.7 1.9 %fusion.4 = bf16[2048,256]{1,0:T(8,128)(2,1)S(1)} fusion(f32[16,256]{1,0:T(8,128)S(1)} %get-tuple-element.57, bf16[2,2048,256]{2,1,0:T(8,128)(2,1)} %collective-permute-done, s32[]{:T(128)S(6)} %select_n.198, f32[16,256]{1,0:T(8,128)S(1)} %get-tuple-element.55, bf16[2,2,2048,256]{3,2,1,0:T(8,128)(2,1)} %bitcast.224, s32[]{:T(128)S(6)} %select_n.199, ...), kind=kLoop, calls=%fused_computation.11 | loop fusion | flops 3145728 | bytes 3178508 | tf_op jit(solution)/shard_map/convert_element_type | solution.py:75
  10.6 3.4 %all-to-all-done = bf16[4,24,2048]{2,1,0:T(8,128)(2,1)S(1)} async-done(((bf16[4,24,2048]{2,1,0:T(8,128)(2,1)}), bf16[4,24,2048]{2,1,0:T(8,128)(2,1)S(1)}, u32[]{:S(2)}, u32[]{:S(2)}) %all-to-all-start) | async-done | bytes 393248 | tf_op jit(solution)/shard_map/all_to_all | solution.py:67
  14.1 3.2 %collective-permute-start.3 = (bf16[4,24,2048]{2,1,0:T(8,128)(2,1)S(1)}, bf16[4,24,2048]{2,1,0:T(8,128)(2,1)S(1)}, u32[]{:S(2)}, u32[]{:S(2)}) collective-permute-start(bf16[4,24,2048]{2,1,0:T(8,128)(2,1)S(1)} %all-to-all-done), channel_id=1, source_target_pairs={{0,12},{4,0},{8,4},{12,8},{1,13},{5,1},{9,5},{13,9},{2,14},{6,2},{... | collective-permute-start | bytes 1179656 | tf_op jit(solution)/shard_map/ppermute | solution.py:21
  17.3 1.8 %collective-permute-start.5 = (bf16[4,24,2048]{2,1,0:T(8,128)(2,1)S(1)}, bf16[4,24,2048]{2,1,0:T(8,128)(2,1)S(1)}, u32[]{:S(2)}, u32[]{:S(2)}) collective-permute-start(bf16[4,24,2048]{2,1,0:T(8,128)(2,1)S(1)} %all-to-all-done), channel_id=1, source_target_pairs={{0,1},{1,2},{2,3},{3,0},{4,5},{5,6},{6,7},{7,4},{8,9},{9,10},{10,1... | collective-permute-start | bytes 1179656 | tf_op jit(solution)/shard_map/ppermute | solution.py:21
  19.1 2.8 %collective-permute-start.6 = (bf16[4,24,2048]{2,1,0:T(8,128)(2,1)S(1)}, bf16[4,24,2048]{2,1,0:T(8,128)(2,1)S(1)}, u32[]{:S(2)}, u32[]{:S(2)}) collective-permute-start(bf16[4,24,2048]{2,1,0:T(8,128)(2,1)S(1)} %all-to-all-done), channel_id=1, source_target_pairs={{0,3},{1,0},{2,1},{3,2},{4,7},{5,4},{6,5},{7,6},{8,11},{9,8},{10,9... | collective-permute-start | bytes 1179656 | tf_op jit(solution)/shard_map/ppermute | solution.py:21
  22.2 3.7 %collective-permute-done.2 = bf16[4,24,2048]{2,1,0:T(8,128)(2,1)S(1)} collective-permute-done((bf16[4,24,2048]{2,1,0:T(8,128)(2,1)S(1)}, bf16[4,24,2048]{2,1,0:T(8,128)(2,1)S(1)}, u32[]{:S(2)}, u32[]{:S(2)}) %collective-permute-start.2) | collective-permute-done | bytes 393248 | tf_op jit(solution)/shard_map/ppermute | solution.py:21
  27.0 13.2 %collective-permute-done.5 = bf16[4,24,2048]{2,1,0:T(8,128)(2,1)S(1)} collective-permute-done((bf16[4,24,2048]{2,1,0:T(8,128)(2,1)S(1)}, bf16[4,24,2048]{2,1,0:T(8,128)(2,1)S(1)}, u32[]{:S(2)}, u32[]{:S(2)}) %collective-permute-start.5) | collective-permute-done | bytes 393248 | tf_op jit(solution)/shard_map/ppermute | solution.py:21
  40.7 2.9 %collective-permute-start.8 = (bf16[8,24,2048]{2,1,0:T(8,128)(2,1)S(1)}, bf16[8,24,2048]{2,1,0:T(8,128)(2,1)S(1)}, u32[]{:S(2)}, u32[]{:S(2)}) collective-permute-start(bf16[8,24,2048]{2,1,0:T(8,128)(2,1)S(1)} %pad_maximum_fusion), channel_id=1, source_target_pairs={{0,12},{4,0},{8,4},{12,8},{1,13},{5,1},{9,5},{13,9},{2,14},{6,2},{... | collective-permute-start | bytes 2359304 | tf_op jit(solution)/shard_map/ppermute | solution.py:21
  43.7 17.8 %collective-permute-done.10 = bf16[2048,256]{1,0:T(8,128)(2,1)S(1)} collective-permute-done((bf16[2048,256]{1,0:T(8,128)(2,1)S(1)}, bf16[2048,256]{1,0:T(8,128)(2,1)S(1)}, u32[]{:S(2)}, u32[]{:S(2)}) %collective-permute-start.10) | collective-permute-done | bytes 1048608 | tf_op jit(solution)/shard_map/ppermute | solution.py:77
  61.6 1.6 collective-permute-start.16
  63.8 2.7 %subtract_convert_fusion = bf16[2048,256]{1,0:T(8,128)(2,1)S(1)} fusion(f32[2048,256]{1,0:T(8,128)S(1)} %copy-done.2, bf16[2048,256]{1,0:T(8,128)(2,1)S(1)} %collective-permute-done.10, bf16[2048,256]{1,0:T(8,128)(2,1)S(1)} %copy-done.3, f32[16,256]{1,0:T(8,128)S(1)} %copy-done.8, bf16[2,2048,256]{2,1,0:T(8,128)(2,1)} %collective-permute-done, ...), kind=kLoop, calls=%fused_computation.13 | loop fusion | flops 8388608 | bytes 7372812 | tf_op jit(solution)/shard_map/convert_element_type | solution.py:89
  66.5 1.7 %collective-permute-start.11 = (bf16[2048,256]{1,0:T(8,128)(2,1)S(1)}, bf16[2048,256]{1,0:T(8,128)(2,1)S(1)}, u32[]{:S(2)}, u32[]{:S(2)}) collective-permute-start(bf16[2048,256]{1,0:T(8,128)(2,1)S(1)} %subtract_convert_fusion), channel_id=1, source_target_pairs={{0,16},{16,32},{32,48},{48,0},{1,17},{17,33},{33,49},{49,1},{2,18}... | collective-permute-start | bytes 3145736 | tf_op jit(solution)/shard_map/ppermute | solution.py:21
  68.3 1.7 %collective-permute-start.14 = (bf16[2048,256]{1,0:T(8,128)(2,1)S(1)}, bf16[2048,256]{1,0:T(8,128)(2,1)S(1)}, u32[]{:S(2)}, u32[]{:S(2)}) collective-permute-start(bf16[2048,256]{1,0:T(8,128)(2,1)S(1)} %subtract_convert_fusion), channel_id=1, source_target_pairs={{0,48},{16,0},{32,16},{48,32},{1,49},{17,1},{33,17},{49,33},{2,50}... | collective-permute-start | bytes 3145736 | tf_op jit(solution)/shard_map/ppermute | solution.py:21
  70.0 4.7 %collective-permute-done.16 = bf16[4,24,2048]{2,1,0:T(8,128)(2,1)S(1)} collective-permute-done((bf16[4,24,2048]{2,1,0:T(8,128)(2,1)S(1)}, bf16[4,24,2048]{2,1,0:T(8,128)(2,1)S(1)}, u32[]{:S(2)}, u32[]{:S(2)}) %collective-permute-start.16) | collective-permute-done | bytes 393248 | tf_op jit(solution)/shard_map/ppermute | solution.py:39
  75.0 2.9 %collective-permute-start.18 = (bf16[4,24,2048]{2,1,0:T(8,128)(2,1)S(1)}, bf16[4,24,2048]{2,1,0:T(8,128)(2,1)S(1)}, u32[]{:S(2)}, u32[]{:S(2)}) collective-permute-start(bf16[4,24,2048]{2,1,0:T(8,128)(2,1)S(1)} %collective-permute-done.16), channel_id=1, source_target_pairs={{0,12},{4,0},{8,4},{12,8},{1,13},{5,1},{9,5},{13,9},{2,14},{6,2},{... | collective-permute-start | bytes 1179656 | tf_op jit(solution)/shard_map/ppermute | solution.py:21
  78.2 1.5 fusion.19
  79.7 13.7 %collective-permute-done.11 = bf16[2048,256]{1,0:T(8,128)(2,1)S(1)} collective-permute-done((bf16[2048,256]{1,0:T(8,128)(2,1)S(1)}, bf16[2048,256]{1,0:T(8,128)(2,1)S(1)}, u32[]{:S(2)}, u32[]{:S(2)}) %collective-permute-start.11) | collective-permute-done | bytes 1048608 | tf_op jit(solution)/shard_map/ppermute | solution.py:21
  93.4 1.5 fusion.16
  96.3 1.6 collective-permute-done.12
  98.2 1.5 fusion.10
  100.2 4.2 %collective-permute-done.19 = bf16[4,24,2048]{2,1,0:T(8,128)(2,1)S(1)} collective-permute-done((bf16[4,24,2048]{2,1,0:T(8,128)(2,1)S(1)}, bf16[4,24,2048]{2,1,0:T(8,128)(2,1)S(1)}, u32[]{:S(2)}, u32[]{:S(2)}) %collective-permute-start.19) | collective-permute-done | bytes 393248 | tf_op jit(solution)/shard_map/ppermute | solution.py:39
  104.7 11.1 %collective-permute-done.13 = f32[24,24,256]{2,1,0:T(8,128)S(1)} collective-permute-done((f32[24,24,256]{2,1,0:T(8,128)S(1)}, f32[24,24,256]{2,1,0:T(8,128)S(1)}, u32[]{:S(2)}, u32[]{:S(2)}) %collective-permute-start.13) | collective-permute-done | bytes 589856 | tf_op jit(solution)/shard_map/ppermute | solution.py:143
  116.6 1.5 convolution_dynamic-update-slice_fusion
  120.6 1.5 copy-done.1
  122.3 1.9 %collective-permute-done.21 = f32[12,24,256]{2,1,0:T(8,128)S(1)} collective-permute-done((f32[12,24,256]{2,1,0:T(8,128)S(1)}, f32[12,24,256]{2,1,0:T(8,128)S(1)}, u32[]{:S(2)}, u32[]{:S(2)}) %collective-permute-start.21) | collective-permute-done | bytes 294944 | tf_op jit(solution)/shard_map/ppermute | solution.py:146
  124.5 3.0 %collective-permute-done.22 = f32[28,2,24,256]{3,2,1,0:T(8,128)} collective-permute-done((f32[28,2,24,256]{3,2,1,0:T(8,128)S(1)}, f32[28,2,24,256]{3,2,1,0:T(8,128)}, u32[]{:S(2)}, u32[]{:S(2)}) %collective-permute-start.22) | collective-permute-done | bytes 1376288 | tf_op jit(solution)/shard_map/ppermute | solution.py:122
  127.5 2.0 %bitcast_add_fusion = f32[28,2,24,256]{3,2,1,0:T(8,128)S(1)} fusion(f32[28,2,24,256]{3,2,1,0:T(8,128)} %collective-permute-done.22, f32[28,2,2,24,256]{4,3,2,1,0:T(8,128)} %copy-done.1, s32[]{:T(128)S(6)} %select_n.200), kind=kLoop, calls=%fused_computation.16 | loop fusion | flops 344064 | bytes 4128772 | tf_op jit(solution)/shard_map/add | solution.py:122
  130.7 16.3 %collective-permute-done.23 = f32[28,24,256]{2,1,0:T(8,128)S(1)} collective-permute-done((f32[28,24,256]{2,1,0:T(8,128)S(1)}, f32[28,24,256]{2,1,0:T(8,128)S(1)}, u32[]{:S(2)}, u32[]{:S(2)}) %collective-permute-start.23) | collective-permute-done | bytes 688160 | tf_op jit(solution)/shard_map/ppermute | solution.py:155
  148.8 14.6 %all_to_all.14 = f32[16,1,72]{2,1,0:T(1,128)S(1)} all-to-all(f32[16,1,72]{2,1,0:T(1,128)S(1)} %bitcast.260), channel_id=1, replica_groups=mesh['zlo'=2,'core'=2,'x'=4,'y'=4,'zhi'=4] {'zhi','y'}, dimensions={0} | all-to-all | bytes 9216 | tf_op jit(solution)/shard_map/all_to_all | solution.py:166
  (129 shorter events, 16.2 us)
Async XLA Ops:
  0.0 124.2 %copy-start = (s32[1,1536]{1,0:T(1,128)S(1)}, s32[1,1536]{1,0:T(1,128)}, u32[]{:S(2)}) copy-start(s32[1,1536]{1,0:T(1,128)} %param.11) | copy-start | bytes 18436
  1.8 4.9 %copy-start.9 = (bf16[1,64,256]{2,1,0:T(8,128)(2,1)S(1)}, bf16[1,64,256]{2,1,0:T(8,128)(2,1)}, u32[]{:S(2)}) copy-start(bf16[1,64,256]{2,1,0:T(8,128)(2,1)} %param.7) | copy-start | bytes 98308
  1.8 6.9 %collective-permute-start = (bf16[2,2048,256]{2,1,0:T(8,128)(2,1)S(1)}, bf16[2,2048,256]{2,1,0:T(8,128)(2,1)}, u32[]{:S(2)}, u32[]{:S(2)}) collective-permute-start(bf16[2,2048,256]{2,1,0:T(8,128)(2,1)S(1)} %dynamic-slice_bitcast_fusion), channel_id=1, source_target_pairs={{0,64},{64,0},{1,65},{65,1},{2,66},{66,2},{3,67},{67,3},{4,68},{68... | collective-permute-start | bytes 6291464 | tf_op jit(solution)/shard_map/ppermute | solution.py:61
  3.2 10.9 %all-to-all-start = ((bf16[4,24,2048]{2,1,0:T(8,128)(2,1)}), bf16[4,24,2048]{2,1,0:T(8,128)(2,1)S(1)}, u32[]{:S(2)}, u32[]{:S(2)}) async-start(bf16[4,24,2048]{2,1,0:T(8,128)(2,1)} %copy.35), calls=%async_computation | async-start | bytes 786432 | tf_op jit(solution)/shard_map/all_to_all | solution.py:67
  6.7 1.4 collective-permute-start.1
  14.1 11.9 %collective-permute-start.2 = (bf16[4,24,2048]{2,1,0:T(8,128)(2,1)S(1)}, bf16[4,24,2048]{2,1,0:T(8,128)(2,1)S(1)}, u32[]{:S(2)}, u32[]{:S(2)}) collective-permute-start(bf16[4,24,2048]{2,1,0:T(8,128)(2,1)S(1)} %all-to-all-done), channel_id=1, source_target_pairs={{0,4},{4,8},{8,12},{12,0},{1,5},{5,9},{9,13},{13,1},{2,6},{6,10},{... | collective-permute-start | bytes 1179656 | tf_op jit(solution)/shard_map/ppermute | solution.py:21
  14.1 11.8 %collective-permute-start.3 = (bf16[4,24,2048]{2,1,0:T(8,128)(2,1)S(1)}, bf16[4,24,2048]{2,1,0:T(8,128)(2,1)S(1)}, u32[]{:S(2)}, u32[]{:S(2)}) collective-permute-start(bf16[4,24,2048]{2,1,0:T(8,128)(2,1)S(1)} %all-to-all-done), channel_id=1, source_target_pairs={{0,12},{4,0},{8,4},{12,8},{1,13},{5,1},{9,5},{13,9},{2,14},{6,2},{... | collective-permute-start | bytes 1179656 | tf_op jit(solution)/shard_map/ppermute | solution.py:21
  17.3 22.9 %collective-permute-start.5 = (bf16[4,24,2048]{2,1,0:T(8,128)(2,1)S(1)}, bf16[4,24,2048]{2,1,0:T(8,128)(2,1)S(1)}, u32[]{:S(2)}, u32[]{:S(2)}) collective-permute-start(bf16[4,24,2048]{2,1,0:T(8,128)(2,1)S(1)} %all-to-all-done), channel_id=1, source_target_pairs={{0,1},{1,2},{2,3},{3,0},{4,5},{5,6},{6,7},{7,4},{8,9},{9,10},{10,1... | collective-permute-start | bytes 1179656 | tf_op jit(solution)/shard_map/ppermute | solution.py:21
  19.1 21.1 %collective-permute-start.6 = (bf16[4,24,2048]{2,1,0:T(8,128)(2,1)S(1)}, bf16[4,24,2048]{2,1,0:T(8,128)(2,1)S(1)}, u32[]{:S(2)}, u32[]{:S(2)}) collective-permute-start(bf16[4,24,2048]{2,1,0:T(8,128)(2,1)S(1)} %all-to-all-done), channel_id=1, source_target_pairs={{0,3},{1,0},{2,1},{3,2},{4,7},{5,4},{6,5},{7,6},{8,11},{9,8},{10,9... | collective-permute-start | bytes 1179656 | tf_op jit(solution)/shard_map/ppermute | solution.py:21
  21.9 39.7 %collective-permute-start.10 = (bf16[2048,256]{1,0:T(8,128)(2,1)S(1)}, bf16[2048,256]{1,0:T(8,128)(2,1)S(1)}, u32[]{:S(2)}, u32[]{:S(2)}) collective-permute-start(bf16[2048,256]{1,0:T(8,128)(2,1)S(1)} %fusion.4), channel_id=1, source_target_pairs={{0,128},{128,0},{1,129},{129,1},{2,130},{130,2},{3,131},{131,3},{4... | collective-permute-start | bytes 3145736 | tf_op jit(solution)/shard_map/ppermute | solution.py:77
  26.0 14.3 %collective-permute-start.4 = (bf16[4,24,2048]{2,1,0:T(8,128)(2,1)S(1)}, bf16[4,24,2048]{2,1,0:T(8,128)(2,1)S(1)}, u32[]{:S(2)}, u32[]{:S(2)}) collective-permute-start(bf16[4,24,2048]{2,1,0:T(8,128)(2,1)S(1)} %broadcast_select_fusion.4), channel_id=1, source_target_pairs={{0,4},{4,8},{8,12},{12,0},{68,64},{72,68},{76,72},{64,76},{1,5},{5... | collective-permute-start | bytes 1179656 | tf_op jit(solution)/shard_map/ppermute | solution.py:39
  40.3 22.9 %collective-permute-start.7 = (bf16[8,24,2048]{2,1,0:T(8,128)(2,1)S(1)}, bf16[8,24,2048]{2,1,0:T(8,128)(2,1)S(1)}, u32[]{:S(2)}, u32[]{:S(2)}) collective-permute-start(bf16[8,24,2048]{2,1,0:T(8,128)(2,1)S(1)} %pad_maximum_fusion), channel_id=1, source_target_pairs={{0,4},{4,8},{8,12},{12,0},{1,5},{5,9},{9,13},{13,1},{2,6},{6,10},{... | collective-permute-start | bytes 2359304 | tf_op jit(solution)/shard_map/ppermute | solution.py:21
  40.7 22.5 %collective-permute-start.8 = (bf16[8,24,2048]{2,1,0:T(8,128)(2,1)S(1)}, bf16[8,24,2048]{2,1,0:T(8,128)(2,1)S(1)}, u32[]{:S(2)}, u32[]{:S(2)}) collective-permute-start(bf16[8,24,2048]{2,1,0:T(8,128)(2,1)S(1)} %pad_maximum_fusion), channel_id=1, source_target_pairs={{0,12},{4,0},{8,4},{12,8},{1,13},{5,1},{9,5},{13,9},{2,14},{6,2},{... | collective-permute-start | bytes 2359304 | tf_op jit(solution)/shard_map/ppermute | solution.py:21
  61.6 2.2 %copy-start.2 = (f32[2048,256]{1,0:T(8,128)S(1)}, f32[2048,256]{1,0:T(8,128)}, u32[]{:S(2)}) copy-start(f32[2048,256]{1,0:T(8,128)} %param.9) | copy-start | bytes 6291460
  61.6 2.2 %copy-start.3 = (bf16[2048,256]{1,0:T(8,128)(2,1)S(1)}, bf16[2048,256]{1,0:T(8,128)(2,1)}, u32[]{:S(2)}) copy-start(bf16[2048,256]{1,0:T(8,128)(2,1)} %param.8) | copy-start | bytes 3145732
  61.6 2.2 %copy-start.7 = (f32[16,256]{1,0:T(8,128)S(1)}, f32[16,256]{1,0:T(8,128)}, u32[]{:S(2)}) copy-start(f32[16,256]{1,0:T(8,128)} %get-tuple-element.54) | copy-start | bytes 49156
  61.6 2.2 %copy-start.8 = (f32[16,256]{1,0:T(8,128)S(1)}, f32[16,256]{1,0:T(8,128)}, u32[]{:S(2)}) copy-start(f32[16,256]{1,0:T(8,128)} %get-tuple-element.56) | copy-start | bytes 49156
  61.6 13.1 %collective-permute-start.16 = (bf16[4,24,2048]{2,1,0:T(8,128)(2,1)S(1)}, bf16[4,24,2048]{2,1,0:T(8,128)(2,1)S(1)}, u32[]{:S(2)}, u32[]{:S(2)}) collective-permute-start(bf16[4,24,2048]{2,1,0:T(8,128)(2,1)S(1)} %broadcast_select_fusion.3), channel_id=1, source_target_pairs={{0,1},{1,2},{2,3},{3,0},{65,64},{66,65},{67,66},{64,67},{4,5},{5,6... | collective-permute-start | bytes 1179656 | tf_op jit(solution)/shard_map/ppermute | solution.py:39
  63.3 14.9 %collective-permute-start.9 = (bf16[8,24,2048]{2,1,0:T(8,128)(2,1)S(1)}, bf16[8,24,2048]{2,1,0:T(8,128)(2,1)S(1)}, u32[]{:S(2)}, u32[]{:S(2)}) collective-permute-start(bf16[8,24,2048]{2,1,0:T(8,128)(2,1)S(1)} %broadcast_select_fusion.1), channel_id=1, source_target_pairs={{0,4},{4,8},{8,12},{12,0},{68,64},{72,68},{76,72},{64,76},{1,5},{5... | collective-permute-start | bytes 2359304 | tf_op jit(solution)/shard_map/ppermute | solution.py:39
  66.5 26.9 %collective-permute-start.11 = (bf16[2048,256]{1,0:T(8,128)(2,1)S(1)}, bf16[2048,256]{1,0:T(8,128)(2,1)S(1)}, u32[]{:S(2)}, u32[]{:S(2)}) collective-permute-start(bf16[2048,256]{1,0:T(8,128)(2,1)S(1)} %subtract_convert_fusion), channel_id=1, source_target_pairs={{0,16},{16,32},{32,48},{48,0},{1,17},{17,33},{33,49},{49,1},{2,18}... | collective-permute-start | bytes 3145736 | tf_op jit(solution)/shard_map/ppermute | solution.py:21
  68.3 27.6 %collective-permute-start.14 = (bf16[2048,256]{1,0:T(8,128)(2,1)S(1)}, bf16[2048,256]{1,0:T(8,128)(2,1)S(1)}, u32[]{:S(2)}, u32[]{:S(2)}) collective-permute-start(bf16[2048,256]{1,0:T(8,128)(2,1)S(1)} %subtract_convert_fusion), channel_id=1, source_target_pairs={{0,48},{16,0},{32,16},{48,32},{1,49},{17,1},{33,17},{49,33},{2,50}... | collective-permute-start | bytes 3145736 | tf_op jit(solution)/shard_map/ppermute | solution.py:21
  74.7 20.6 %collective-permute-start.17 = (bf16[4,24,2048]{2,1,0:T(8,128)(2,1)S(1)}, bf16[4,24,2048]{2,1,0:T(8,128)(2,1)S(1)}, u32[]{:S(2)}, u32[]{:S(2)}) collective-permute-start(bf16[4,24,2048]{2,1,0:T(8,128)(2,1)S(1)} %collective-permute-done.16), channel_id=1, source_target_pairs={{0,4},{4,8},{8,12},{12,0},{1,5},{5,9},{9,13},{13,1},{2,6},{6,10},{... | collective-permute-start | bytes 1179656 | tf_op jit(solution)/shard_map/ppermute | solution.py:21
  75.0 20.3 %collective-permute-start.18 = (bf16[4,24,2048]{2,1,0:T(8,128)(2,1)S(1)}, bf16[4,24,2048]{2,1,0:T(8,128)(2,1)S(1)}, u32[]{:S(2)}, u32[]{:S(2)}) collective-permute-start(bf16[4,24,2048]{2,1,0:T(8,128)(2,1)S(1)} %collective-permute-done.16), channel_id=1, source_target_pairs={{0,12},{4,0},{8,4},{12,8},{1,13},{5,1},{9,5},{13,9},{2,14},{6,2},{... | collective-permute-start | bytes 1179656 | tf_op jit(solution)/shard_map/ppermute | solution.py:21
  95.0 2.9 %collective-permute-start.12 = (f32[24,2,24,256]{3,2,1,0:T(8,128)S(1)}, f32[24,2,24,256]{3,2,1,0:T(8,128)S(1)}, u32[]{:S(2)}, u32[]{:S(2)}) collective-permute-start(f32[24,2,24,256]{3,2,1,0:T(8,128)S(1)} %fusion.9), channel_id=1, source_target_pairs={{0,64},{64,0},{1,65},{65,1},{2,66},{66,2},{3,67},{67,3},{4,68},{68... | collective-permute-start | bytes 3538952 | tf_op jit(solution)/shard_map/ppermute | solution.py:122
  95.4 9.1 %collective-permute-start.19 = (bf16[4,24,2048]{2,1,0:T(8,128)(2,1)S(1)}, bf16[4,24,2048]{2,1,0:T(8,128)(2,1)S(1)}, u32[]{:S(2)}, u32[]{:S(2)}) collective-permute-start(bf16[4,24,2048]{2,1,0:T(8,128)(2,1)S(1)} %broadcast_select_fusion.2), channel_id=1, source_target_pairs={{0,4},{4,8},{8,12},{12,0},{68,64},{72,68},{76,72},{64,76},{1,5},{5... | collective-permute-start | bytes 1179656 | tf_op jit(solution)/shard_map/ppermute | solution.py:39
  96.0 20.6 %collective-permute-start.15 = (bf16[2048,256]{1,0:T(8,128)(2,1)S(1)}, bf16[2048,256]{1,0:T(8,128)(2,1)S(1)}, u32[]{:S(2)}, u32[]{:S(2)}) collective-permute-start(bf16[2048,256]{1,0:T(8,128)(2,1)S(1)} %broadcast_select_fusion), channel_id=1, source_target_pairs={{0,16},{16,32},{32,48},{48,0},{80,64},{96,80},{112,96},{64,112},{1... | collective-permute-start | bytes 3145736 | tf_op jit(solution)/shard_map/ppermute | solution.py:39
  99.8 4.8 %collective-permute-start.20 = (f32[12,2,24,256]{3,2,1,0:T(8,128)S(1)}, f32[12,2,24,256]{3,2,1,0:T(8,128)S(1)}, u32[]{:S(2)}, u32[]{:S(2)}) collective-permute-start(f32[12,2,24,256]{3,2,1,0:T(8,128)S(1)} %dynamic-slice_bitcast_fusion.3), channel_id=1, source_target_pairs={{0,64},{64,0},{1,65},{65,1},{2,66},{66,2},{3,67},{67,3},{4,68},{68... | collective-permute-start | bytes 1769480 | tf_op jit(solution)/shard_map/ppermute | solution.py:122
  100.1 15.6 %collective-permute-start.13 = (f32[24,24,256]{2,1,0:T(8,128)S(1)}, f32[24,24,256]{2,1,0:T(8,128)S(1)}, u32[]{:S(2)}, u32[]{:S(2)}) collective-permute-start(f32[24,24,256]{2,1,0:T(8,128)S(1)} %dynamic-slice_bitcast_fusion.4), channel_id=1, source_target_pairs={{0,128},{128,0},{1,129},{129,1},{2,130},{130,2},{3,131},{131,3},{4... | collective-permute-start | bytes 1769480 | tf_op jit(solution)/shard_map/ppermute | solution.py:143
  115.8 8.4 %collective-permute-start.21 = (f32[12,24,256]{2,1,0:T(8,128)S(1)}, f32[12,24,256]{2,1,0:T(8,128)S(1)}, u32[]{:S(2)}, u32[]{:S(2)}) collective-permute-start(f32[12,24,256]{2,1,0:T(8,128)S(1)} %dynamic-slice_bitcast_fusion.5), channel_id=1, source_target_pairs={{0,128},{128,0},{1,129},{129,1},{2,130},{130,2},{3,131},{131,3},{4... | collective-permute-start | bytes 884744 | tf_op jit(solution)/shard_map/ppermute | solution.py:146
  124.2 3.3 %collective-permute-start.22 = (f32[28,2,24,256]{3,2,1,0:T(8,128)S(1)}, f32[28,2,24,256]{3,2,1,0:T(8,128)}, u32[]{:S(2)}, u32[]{:S(2)}) collective-permute-start(f32[28,2,24,256]{3,2,1,0:T(8,128)S(1)} %dynamic-slice_bitcast_fusion.1), channel_id=1, source_target_pairs={{0,64},{64,0},{1,65},{65,1},{2,66},{66,2},{3,67},{67,3},{4,68},{68... | collective-permute-start | bytes 4128776 | tf_op jit(solution)/shard_map/ppermute | solution.py:122
  124.5 5.7 %copy-start.5 = (f32[24,24,256]{2,1,0:T(8,128)S(1)}, f32[24,24,256]{2,1,0:T(8,128)}, u32[]{:S(2)}) copy-start(f32[24,24,256]{2,1,0:T(8,128)} %copy-done.4) | copy-start | bytes 1769476
  129.5 17.6 %collective-permute-start.23 = (f32[28,24,256]{2,1,0:T(8,128)S(1)}, f32[28,24,256]{2,1,0:T(8,128)S(1)}, u32[]{:S(2)}, u32[]{:S(2)}) collective-permute-start(f32[28,24,256]{2,1,0:T(8,128)S(1)} %dynamic-slice_bitcast_fusion.2), channel_id=1, source_target_pairs={{0,128},{128,0},{1,129},{129,1},{2,130},{130,2},{3,131},{131,3},{4... | collective-permute-start | bytes 2064392 | tf_op jit(solution)/shard_map/ppermute | solution.py:155
  (3 other events, 4.3 us)
